TPU v7x, 512 devices: a whole 4x4x16 slice. The times are simulated.
512 devices in a mesh: ka: 16 (over z_lo, core), tau: 32 (over y, z_hi, x).
Axes of the slice: x: 4, y: 4, z: 16 (z_hi: 2, z_lo: 8; z = z_hi * 8 + z_lo), core: 2. Of those that a mesh axis runs over, the one named last changes fastest.
Arguments:
- bcoef: bfloat16 [16, 16, 384, 384], P('ka', None, 'tau'), may hold values from -0.3125 to 0.3125
- fwd_green: bfloat16 [16, 32, 384, 384], P('ka', 'tau'), may hold values from -0.3125 to 0.3125
- back_green: bfloat16 [16, 32, 384, 384], P('ka', 'tau'), may hold values from -0.3125 to 0.3125
- kmq: int32 [16], P('ka'), may hold values from 0 to 15, as said below
- ir_table: float32 [2, 128, 32], replicated, may hold values from -6 to 6
- ir_fit: float32 [32, 32], replicated, may hold values from -1 to 1
- freq_index: int32 [32], replicated, may hold values from 0 to 127
Outputs:
- polar_freq: float32 [2, 32, 16, 16], P(None, 'tau', 'ka')
Inputs may be any that keep to these rules, and one draw needn't show every extreme that they name: kmq[k] is the index of k - q on a 4 x 4 grid of k-points numbered row by row with wrap-around, for one q whose two components are both nonzero (each 1 to 3); it is a permutation.
All inputs are finite; a program needn't handle non-finite values.
Results may differ from a plain program's by a relative error of at most 0.004.
Values may be sent and summed in bfloat16 or wider, within the bound.
No kernel may reach another device: no remote copies, remote signals or barrier semaphores. Data moves between devices by JAX's collectives and lax.ppermute only.
A program may use at most 64 MiB of HBM per device.

v0:
```python
import jax
import jax.numpy as jnp
from jax import lax
from jax.sharding import PartitionSpec as P


def shifted(block, axis, distance):
    devices = range(lax.axis_size(axis))
    route = [((i - distance) % len(devices), i) for i in devices]
    return lax.ppermute(block, axis, route)


def follow_line(back_green, target):
    count = lax.axis_size("ka")
    own = lax.axis_index("ka")
    offset = (own - target) % count

    def advance(step, carried):
        moving, result = carried
        moving = shifted(moving, "ka", 1)
        result = jnp.where(offset == step, moving, result)
        return (moving, result)

    moving, result = lax.fori_loop(1, count, advance, (back_green, back_green))
    return result[0, 0]


def shards(bcoef, fwd_green, back_green, kmq, ir_table, ir_fit, freq_index):
    orb_width = fwd_green.shape[-1]
    blocks = bcoef.shape[1]
    green_fwd = fwd_green[0, 0]
    shard_rows = lax.all_gather(bcoef, "tau", axis=2, tiled=True)
    stacked_rows = shard_rows.reshape(-1, orb_width)
    product = jnp.dot(stacked_rows, green_fwd, preferred_element_type=jnp.float32)
    product = product.astype(jnp.bfloat16).reshape(shard_rows.shape)
    joined = jnp.stack([shard_rows, product], axis=0)
    coef_full = joined[0, 0]
    left_side = joined[1, 0]
    target = kmq[0]
    green_back = follow_line(back_green, target)
    right_side = jnp.einsum(
        "mi,qml->qil", green_back, coef_full, preferred_element_type=jnp.float32
    ).astype(jnp.bfloat16)
    polar_time = lax.dot_general(
        left_side.reshape(blocks, -1),
        right_side.reshape(blocks, -1),
        (((1,), (1,)), ((), ())),
        preferred_element_type=jnp.float32,
    )
    polar_time = polar_time * (-1.0 / lax.axis_size("ka"))
    candidates = ir_table.shape[1]
    selector = (freq_index[:, None] == jnp.arange(candidates, dtype=jnp.int32)[None, :]).astype(
        jnp.float32
    )
    chosen = jnp.einsum("wn,cnl->cwl", selector, ir_table, precision=lax.Precision.HIGHEST)
    transform = jnp.einsum("cwl,lt->cwt", chosen, ir_fit, precision=lax.Precision.HIGHEST)
    entries = polar_time.reshape(1, blocks * blocks)
    columns = lax.all_to_all(entries, "tau", split_axis=1, concat_axis=0, tiled=True)
    freq_cols = jnp.einsum("cwt,te->cwe", transform, columns, precision=lax.Precision.HIGHEST)
    regrouped = lax.all_to_all(freq_cols, "tau", split_axis=1, concat_axis=2, tiled=True)
    regrouped = regrouped.reshape(2, -1, blocks, blocks)
    return lax.psum_scatter(regrouped, "ka", scatter_dimension=2, tiled=True)


def solution(mesh):
    return jax.shard_map(
        shards,
        mesh=mesh,
        in_specs=(
            P("ka", None, "tau", None),
            P("ka", "tau", None, None),
            P("ka", "tau", None, None),
            P("ka"),
            P(),
            P(),
            P(),
        ),
        out_specs=P(None, "tau", "ka", None),
        check_vma=False,
    )
```

profile of v0, /device:TPU:1, one launch (start us, length us, event | category | flops | bytes accessed | tf_op | source)
XLA Modules:
  0.0 470.1 jit_solution(13150969642897817824)
XLA Ops:
  9.3 257.2 %while.15 = (s32[]{:T(128)}, bf16[1,1,384,384]{3,2,1,0:T(8,128)(2,1)S(1)}, bf16[1,1,384,384]{3,2,1,0:T(8,128)(2,1)S(1)}, s32[]{:T(128)}, s32[]{:T(128)}) while((s32[]{:T(128)}, bf16[1,1,384,384]{3,2,1,0:T(8,128)(2,1)S(1)}, bf16[1,1,384,384]{3,2,1,0:T(8,128)(2,1)S(1)}, s32[]{:T(128)}, s32[]{:T(128)}) %tuple.28), condition=%wide.region_1.2_spmd, body=%wide.region_0.1_spmd.sunk | while | flops 147459 | bytes 2654319 | solution.py:24
  9.3 4.9 %collective-permute-start = (bf16[1,1,384,384]{3,2,1,0:T(8,128)(2,1)S(1)}, bf16[1,1,384,384]{3,2,1,0:T(8,128)(2,1)S(1)}, u32[]{:S(2)}, u32[]{:S(2)}) collective-permute-start(bf16[1,1,384,384]{3,2,1,0:T(8,128)(2,1)S(1)} %get-tuple-element.124), channel_id=1, source_target_pairs={{480,0},{0,32},{32,64},{64,96},{96,128},{128,160},{160,192},{192,2... | collective-permute-start | bytes 884744 | tf_op jit(solution)/shard_map/while/body/eval_jaxpr/ppermute | solution.py:10
  14.3 4.9 %collective-permute-done = bf16[1,1,384,384]{3,2,1,0:T(8,128)(2,1)S(1)} collective-permute-done((bf16[1,1,384,384]{3,2,1,0:T(8,128)(2,1)S(1)}, bf16[1,1,384,384]{3,2,1,0:T(8,128)(2,1)S(1)}, u32[]{:S(2)}, u32[]{:S(2)}) %collective-permute-start) | collective-permute-done | bytes 294944 | tf_op jit(solution)/shard_map/while/body/eval_jaxpr/ppermute | solution.py:10
  19.3 3.1 collective-permute-start
  22.5 11.5 %collective-permute-done = bf16[1,1,384,384]{3,2,1,0:T(8,128)(2,1)S(1)} collective-permute-done((bf16[1,1,384,384]{3,2,1,0:T(8,128)(2,1)S(1)}, bf16[1,1,384,384]{3,2,1,0:T(8,128)(2,1)S(1)}, u32[]{:S(2)}, u32[]{:S(2)}) %collective-permute-start) | collective-permute-done | bytes 294944 | tf_op jit(solution)/shard_map/while/body/eval_jaxpr/ppermute | solution.py:10
  34.2 1.9 collective-permute-start
  36.1 12.8 %collective-permute-done = bf16[1,1,384,384]{3,2,1,0:T(8,128)(2,1)S(1)} collective-permute-done((bf16[1,1,384,384]{3,2,1,0:T(8,128)(2,1)S(1)}, bf16[1,1,384,384]{3,2,1,0:T(8,128)(2,1)S(1)}, u32[]{:S(2)}, u32[]{:S(2)}) %collective-permute-start) | collective-permute-done | bytes 294944 | tf_op jit(solution)/shard_map/while/body/eval_jaxpr/ppermute | solution.py:10
  51.0 12.7 %collective-permute-done = bf16[1,1,384,384]{3,2,1,0:T(8,128)(2,1)S(1)} collective-permute-done((bf16[1,1,384,384]{3,2,1,0:T(8,128)(2,1)S(1)}, bf16[1,1,384,384]{3,2,1,0:T(8,128)(2,1)S(1)}, u32[]{:S(2)}, u32[]{:S(2)}) %collective-permute-start) | collective-permute-done | bytes 294944 | tf_op jit(solution)/shard_map/while/body/eval_jaxpr/ppermute | solution.py:10
  65.8 12.9 %collective-permute-done = bf16[1,1,384,384]{3,2,1,0:T(8,128)(2,1)S(1)} collective-permute-done((bf16[1,1,384,384]{3,2,1,0:T(8,128)(2,1)S(1)}, bf16[1,1,384,384]{3,2,1,0:T(8,128)(2,1)S(1)}, u32[]{:S(2)}, u32[]{:S(2)}) %collective-permute-start) | collective-permute-done | bytes 294944 | tf_op jit(solution)/shard_map/while/body/eval_jaxpr/ppermute | solution.py:10
  80.8 15.3 %collective-permute-done = bf16[1,1,384,384]{3,2,1,0:T(8,128)(2,1)S(1)} collective-permute-done((bf16[1,1,384,384]{3,2,1,0:T(8,128)(2,1)S(1)}, bf16[1,1,384,384]{3,2,1,0:T(8,128)(2,1)S(1)}, u32[]{:S(2)}, u32[]{:S(2)}) %collective-permute-start) | collective-permute-done | bytes 294944 | tf_op jit(solution)/shard_map/while/body/eval_jaxpr/ppermute | solution.py:10
  98.2 12.7 %collective-permute-done = bf16[1,1,384,384]{3,2,1,0:T(8,128)(2,1)S(1)} collective-permute-done((bf16[1,1,384,384]{3,2,1,0:T(8,128)(2,1)S(1)}, bf16[1,1,384,384]{3,2,1,0:T(8,128)(2,1)S(1)}, u32[]{:S(2)}, u32[]{:S(2)}) %collective-permute-start) | collective-permute-done | bytes 294944 | tf_op jit(solution)/shard_map/while/body/eval_jaxpr/ppermute | solution.py:10
  113.1 12.9 %collective-permute-done = bf16[1,1,384,384]{3,2,1,0:T(8,128)(2,1)S(1)} collective-permute-done((bf16[1,1,384,384]{3,2,1,0:T(8,128)(2,1)S(1)}, bf16[1,1,384,384]{3,2,1,0:T(8,128)(2,1)S(1)}, u32[]{:S(2)}, u32[]{:S(2)}) %collective-permute-start) | collective-permute-done | bytes 294944 | tf_op jit(solution)/shard_map/while/body/eval_jaxpr/ppermute | solution.py:10
  128.1 26.8 %collective-permute-done = bf16[1,1,384,384]{3,2,1,0:T(8,128)(2,1)S(1)} collective-permute-done((bf16[1,1,384,384]{3,2,1,0:T(8,128)(2,1)S(1)}, bf16[1,1,384,384]{3,2,1,0:T(8,128)(2,1)S(1)}, u32[]{:S(2)}, u32[]{:S(2)}) %collective-permute-start) | collective-permute-done | bytes 294944 | tf_op jit(solution)/shard_map/while/body/eval_jaxpr/ppermute | solution.py:10
  155.1 5.7 %collective-permute-start = (bf16[1,1,384,384]{3,2,1,0:T(8,128)(2,1)S(1)}, bf16[1,1,384,384]{3,2,1,0:T(8,128)(2,1)S(1)}, u32[]{:S(2)}, u32[]{:S(2)}) collective-permute-start(bf16[1,1,384,384]{3,2,1,0:T(8,128)(2,1)S(1)} %get-tuple-element.124), channel_id=1, source_target_pairs={{480,0},{0,32},{32,64},{64,96},{96,128},{128,160},{160,192},{192,2... | collective-permute-start | bytes 884744 | tf_op jit(solution)/shard_map/while/body/eval_jaxpr/ppermute | solution.py:10
  160.7 23.2 %collective-permute-done = bf16[1,1,384,384]{3,2,1,0:T(8,128)(2,1)S(1)} collective-permute-done((bf16[1,1,384,384]{3,2,1,0:T(8,128)(2,1)S(1)}, bf16[1,1,384,384]{3,2,1,0:T(8,128)(2,1)S(1)}, u32[]{:S(2)}, u32[]{:S(2)}) %collective-permute-start) | collective-permute-done | bytes 294944 | tf_op jit(solution)/shard_map/while/body/eval_jaxpr/ppermute | solution.py:10
  184.1 4.7 collective-permute-start
  188.8 18.3 %collective-permute-done = bf16[1,1,384,384]{3,2,1,0:T(8,128)(2,1)S(1)} collective-permute-done((bf16[1,1,384,384]{3,2,1,0:T(8,128)(2,1)S(1)}, bf16[1,1,384,384]{3,2,1,0:T(8,128)(2,1)S(1)}, u32[]{:S(2)}, u32[]{:S(2)}) %collective-permute-start) | collective-permute-done | bytes 294944 | tf_op jit(solution)/shard_map/while/body/eval_jaxpr/ppermute | solution.py:10
  209.2 12.7 %collective-permute-done = bf16[1,1,384,384]{3,2,1,0:T(8,128)(2,1)S(1)} collective-permute-done((bf16[1,1,384,384]{3,2,1,0:T(8,128)(2,1)S(1)}, bf16[1,1,384,384]{3,2,1,0:T(8,128)(2,1)S(1)}, u32[]{:S(2)}, u32[]{:S(2)}) %collective-permute-start) | collective-permute-done | bytes 294944 | tf_op jit(solution)/shard_map/while/body/eval_jaxpr/ppermute | solution.py:10
  224.0 12.7 %collective-permute-done = bf16[1,1,384,384]{3,2,1,0:T(8,128)(2,1)S(1)} collective-permute-done((bf16[1,1,384,384]{3,2,1,0:T(8,128)(2,1)S(1)}, bf16[1,1,384,384]{3,2,1,0:T(8,128)(2,1)S(1)}, u32[]{:S(2)}, u32[]{:S(2)}) %collective-permute-start) | collective-permute-done | bytes 294944 | tf_op jit(solution)/shard_map/while/body/eval_jaxpr/ppermute | solution.py:10
  236.9 1.9 collective-permute-start
  238.9 12.7 %collective-permute-done = bf16[1,1,384,384]{3,2,1,0:T(8,128)(2,1)S(1)} collective-permute-done((bf16[1,1,384,384]{3,2,1,0:T(8,128)(2,1)S(1)}, bf16[1,1,384,384]{3,2,1,0:T(8,128)(2,1)S(1)}, u32[]{:S(2)}, u32[]{:S(2)}) %collective-permute-start) | collective-permute-done | bytes 294944 | tf_op jit(solution)/shard_map/while/body/eval_jaxpr/ppermute | solution.py:10
  253.7 12.7 %collective-permute-done = bf16[1,1,384,384]{3,2,1,0:T(8,128)(2,1)S(1)} collective-permute-done((bf16[1,1,384,384]{3,2,1,0:T(8,128)(2,1)S(1)}, bf16[1,1,384,384]{3,2,1,0:T(8,128)(2,1)S(1)}, u32[]{:S(2)}, u32[]{:S(2)}) %collective-permute-start) | collective-permute-done | bytes 294944 | tf_op jit(solution)/shard_map/while/body/eval_jaxpr/ppermute | solution.py:10
  266.6 5.3 %fusion.2 = bf16[384,16,384]{2,0,1:T(8,128)(2,1)S(1)} fusion(bf16[1,1,384,384]{3,2,1,0:T(8,128)(2,1)S(1)} %get-tuple-element.84, bf16[1,16,384,384]{3,1,0,2:T(8,128)(2,1)} %all-gather.2.cloned.1.call-done), kind=kOutput, calls=%fused_computation.4 | convolution fusion | flops 1814298624 | bytes 9732096 | tf_op jit(solution)/shard_map/mi,qml->qil/dot_general | solution.py:41
  271.9 5.0 %copy.37 = bf16[2,8,384,384]{3,1,2,0:T(8,128)(2,1)} copy(bf16[2,8,384,384]{3,2,1,0:T(8,128)(2,1)S(1)} %bitcast.43) | data formatting | bytes 9437184
  278.0 4.7 %convolution_convert_fusion = bf16[6144,384]{1,0:T(8,128)(2,1)} fusion(bf16[6144,384]{1,0:T(8,128)(2,1)S(1)} %bitcast.41, bf16[1,1,384,384]{3,2,1,0:T(8,128)(2,1)S(1)} %copy-done), kind=kOutput, calls=%fused_computation.1 | convolution fusion | flops 1814298624 | bytes 9732096 | tf_op jit(solution)/shard_map/dot_general | solution.py:34
  282.7 5.2 %reshape_squeeze_stack_reshape.3 = bf16[16,147456]{1,0:T(8,128)(2,1)} reshape(bf16[6144,384]{1,0:T(8,128)(2,1)} %convolution_convert_fusion) | data formatting | bytes 9437184 | tf_op jit(solution)/shard_map/reshape;squeeze;stack;reshape | solution.py:45
  288.0 5.9 %convolution_multiply_fusion = f32[16,16]{1,0:T(8,128)S(1)} fusion(bf16[16,147456]{1,0:T(8,128)(2,1)} %reshape_squeeze_stack_reshape.3, bf16[16,147456]{1,0:T(8,128)(2,1)} %bitcast.42), kind=kOutput, calls=%fused_computation.6 | convolution fusion | flops 75497728 | bytes 9438208 | tf_op jit(solution)/shard_map/dot_general | solution.py:44
  294.5 36.7 %all-to-all-start = ((f32[1,32,8]{2,0,1:T(1,128)}), f32[1,32,8]{2,0,1:T(1,128)S(1)}, u32[]{:S(2)}, u32[]{:S(2)}) async-start(f32[1,32,8]{2,0,1:T(1,128)} %bitcast.11), calls=%async_computation | async-start | bytes 32768 | tf_op jit(solution)/shard_map/all_to_all | solution.py:58
  331.4 15.7 %all-to-all-done = f32[1,32,8]{2,0,1:T(1,128)S(1)} async-done(((f32[1,32,8]{2,0,1:T(1,128)}), f32[1,32,8]{2,0,1:T(1,128)S(1)}, u32[]{:S(2)}, u32[]{:S(2)}) %all-to-all-start) | async-done | bytes 1056 | tf_op jit(solution)/shard_map/all_to_all | solution.py:58
  348.0 3.8 all-to-all-start.1
  353.2 14.6 %all-to-all-done.1 = f32[2,32,8]{2,0,1:T(2,128)S(1)} async-done(((f32[2,32,8]{2,0,1:T(2,128)}), f32[2,32,8]{2,0,1:T(2,128)S(1)}, u32[]{:S(2)}, u32[]{:S(2)}) %all-to-all-start.1) | async-done | bytes 2080 | tf_op jit(solution)/shard_map/all_to_all | solution.py:60
  367.9 94.2 %all-reduce = f32[2,1,16,16]{3,0,1,2:T(2,128)S(1)} all-reduce(f32[2,1,16,16]{3,0,1,2:T(2,128)S(1)} %copy.33), channel_id=2, replica_groups=mesh['ka'=16,'tau'=32] {'ka'}, use_global_device_ids=true, to_apply=%region_2.3.clone | all-reduce | flops 512 | bytes 4096
  (61 shorter events, 27.2 us)
Async XLA Ops:
  6.5 271.5 %copy-start = (bf16[1,1,384,384]{3,2,1,0:T(8,128)(2,1)S(1)}, bf16[1,1,384,384]{3,2,1,0:T(8,128)(2,1)}, u32[]{:S(2)}) copy-start(bf16[1,1,384,384]{3,2,1,0:T(8,128)(2,1)} %param.10) | copy-start | bytes 884740
  6.5 260.0 %all-gather.2.cloned.1.call-start = ((), (), s32[]{:S(2)}) async-start(), calls=%async_computation.2 | async-start | bytes 4866048 | tf_op jit(solution)/shard_map/all_gather | solution.py:32
  9.3 9.9 %collective-permute-start = (bf16[1,1,384,384]{3,2,1,0:T(8,128)(2,1)S(1)}, bf16[1,1,384,384]{3,2,1,0:T(8,128)(2,1)S(1)}, u32[]{:S(2)}, u32[]{:S(2)}) collective-permute-start(bf16[1,1,384,384]{3,2,1,0:T(8,128)(2,1)S(1)} %get-tuple-element.124), channel_id=1, source_target_pairs={{480,0},{0,32},{32,64},{64,96},{96,128},{128,160},{160,192},{192,2... | collective-permute-start | bytes 884744 | tf_op jit(solution)/shard_map/while/body/eval_jaxpr/ppermute | solution.py:10
  19.3 14.6 %collective-permute-start = (bf16[1,1,384,384]{3,2,1,0:T(8,128)(2,1)S(1)}, bf16[1,1,384,384]{3,2,1,0:T(8,128)(2,1)S(1)}, u32[]{:S(2)}, u32[]{:S(2)}) collective-permute-start(bf16[1,1,384,384]{3,2,1,0:T(8,128)(2,1)S(1)} %get-tuple-element.124), channel_id=1, source_target_pairs={{480,0},{0,32},{32,64},{64,96},{96,128},{128,160},{160,192},{192,2... | collective-permute-start | bytes 884744 | tf_op jit(solution)/shard_map/while/body/eval_jaxpr/ppermute | solution.py:10
  34.2 14.7 %collective-permute-start = (bf16[1,1,384,384]{3,2,1,0:T(8,128)(2,1)S(1)}, bf16[1,1,384,384]{3,2,1,0:T(8,128)(2,1)S(1)}, u32[]{:S(2)}, u32[]{:S(2)}) collective-permute-start(bf16[1,1,384,384]{3,2,1,0:T(8,128)(2,1)S(1)} %get-tuple-element.124), channel_id=1, source_target_pairs={{480,0},{0,32},{32,64},{64,96},{96,128},{128,160},{160,192},{192,2... | collective-permute-start | bytes 884744 | tf_op jit(solution)/shard_map/while/body/eval_jaxpr/ppermute | solution.py:10
  49.1 14.6 %collective-permute-start = (bf16[1,1,384,384]{3,2,1,0:T(8,128)(2,1)S(1)}, bf16[1,1,384,384]{3,2,1,0:T(8,128)(2,1)S(1)}, u32[]{:S(2)}, u32[]{:S(2)}) collective-permute-start(bf16[1,1,384,384]{3,2,1,0:T(8,128)(2,1)S(1)} %get-tuple-element.124), channel_id=1, source_target_pairs={{480,0},{0,32},{32,64},{64,96},{96,128},{128,160},{160,192},{192,2... | collective-permute-start | bytes 884744 | tf_op jit(solution)/shard_map/while/body/eval_jaxpr/ppermute | solution.py:10
  63.9 14.8 %collective-permute-start = (bf16[1,1,384,384]{3,2,1,0:T(8,128)(2,1)S(1)}, bf16[1,1,384,384]{3,2,1,0:T(8,128)(2,1)S(1)}, u32[]{:S(2)}, u32[]{:S(2)}) collective-permute-start(bf16[1,1,384,384]{3,2,1,0:T(8,128)(2,1)S(1)} %get-tuple-element.124), channel_id=1, source_target_pairs={{480,0},{0,32},{32,64},{64,96},{96,128},{128,160},{160,192},{192,2... | collective-permute-start | bytes 884744 | tf_op jit(solution)/shard_map/while/body/eval_jaxpr/ppermute | solution.py:10
  78.9 17.2 %collective-permute-start = (bf16[1,1,384,384]{3,2,1,0:T(8,128)(2,1)S(1)}, bf16[1,1,384,384]{3,2,1,0:T(8,128)(2,1)S(1)}, u32[]{:S(2)}, u32[]{:S(2)}) collective-permute-start(bf16[1,1,384,384]{3,2,1,0:T(8,128)(2,1)S(1)} %get-tuple-element.124), channel_id=1, source_target_pairs={{480,0},{0,32},{32,64},{64,96},{96,128},{128,160},{160,192},{192,2... | collective-permute-start | bytes 884744 | tf_op jit(solution)/shard_map/while/body/eval_jaxpr/ppermute | solution.py:10
  96.3 14.6 %collective-permute-start = (bf16[1,1,384,384]{3,2,1,0:T(8,128)(2,1)S(1)}, bf16[1,1,384,384]{3,2,1,0:T(8,128)(2,1)S(1)}, u32[]{:S(2)}, u32[]{:S(2)}) collective-permute-start(bf16[1,1,384,384]{3,2,1,0:T(8,128)(2,1)S(1)} %get-tuple-element.124), channel_id=1, source_target_pairs={{480,0},{0,32},{32,64},{64,96},{96,128},{128,160},{160,192},{192,2... | collective-permute-start | bytes 884744 | tf_op jit(solution)/shard_map/while/body/eval_jaxpr/ppermute | solution.py:10
  111.1 14.8 %collective-permute-start = (bf16[1,1,384,384]{3,2,1,0:T(8,128)(2,1)S(1)}, bf16[1,1,384,384]{3,2,1,0:T(8,128)(2,1)S(1)}, u32[]{:S(2)}, u32[]{:S(2)}) collective-permute-start(bf16[1,1,384,384]{3,2,1,0:T(8,128)(2,1)S(1)} %get-tuple-element.124), channel_id=1, source_target_pairs={{480,0},{0,32},{32,64},{64,96},{96,128},{128,160},{160,192},{192,2... | collective-permute-start | bytes 884744 | tf_op jit(solution)/shard_map/while/body/eval_jaxpr/ppermute | solution.py:10
  126.1 28.7 %collective-permute-start = (bf16[1,1,384,384]{3,2,1,0:T(8,128)(2,1)S(1)}, bf16[1,1,384,384]{3,2,1,0:T(8,128)(2,1)S(1)}, u32[]{:S(2)}, u32[]{:S(2)}) collective-permute-start(bf16[1,1,384,384]{3,2,1,0:T(8,128)(2,1)S(1)} %get-tuple-element.124), channel_id=1, source_target_pairs={{480,0},{0,32},{32,64},{64,96},{96,128},{128,160},{160,192},{192,2... | collective-permute-start | bytes 884744 | tf_op jit(solution)/shard_map/while/body/eval_jaxpr/ppermute | solution.py:10
  155.1 28.9 %collective-permute-start = (bf16[1,1,384,384]{3,2,1,0:T(8,128)(2,1)S(1)}, bf16[1,1,384,384]{3,2,1,0:T(8,128)(2,1)S(1)}, u32[]{:S(2)}, u32[]{:S(2)}) collective-permute-start(bf16[1,1,384,384]{3,2,1,0:T(8,128)(2,1)S(1)} %get-tuple-element.124), channel_id=1, source_target_pairs={{480,0},{0,32},{32,64},{64,96},{96,128},{128,160},{160,192},{192,2... | collective-permute-start | bytes 884744 | tf_op jit(solution)/shard_map/while/body/eval_jaxpr/ppermute | solution.py:10
  184.1 23.0 %collective-permute-start = (bf16[1,1,384,384]{3,2,1,0:T(8,128)(2,1)S(1)}, bf16[1,1,384,384]{3,2,1,0:T(8,128)(2,1)S(1)}, u32[]{:S(2)}, u32[]{:S(2)}) collective-permute-start(bf16[1,1,384,384]{3,2,1,0:T(8,128)(2,1)S(1)} %get-tuple-element.124), channel_id=1, source_target_pairs={{480,0},{0,32},{32,64},{64,96},{96,128},{128,160},{160,192},{192,2... | collective-permute-start | bytes 884744 | tf_op jit(solution)/shard_map/while/body/eval_jaxpr/ppermute | solution.py:10
  207.3 14.6 %collective-permute-start = (bf16[1,1,384,384]{3,2,1,0:T(8,128)(2,1)S(1)}, bf16[1,1,384,384]{3,2,1,0:T(8,128)(2,1)S(1)}, u32[]{:S(2)}, u32[]{:S(2)}) collective-permute-start(bf16[1,1,384,384]{3,2,1,0:T(8,128)(2,1)S(1)} %get-tuple-element.124), channel_id=1, source_target_pairs={{480,0},{0,32},{32,64},{64,96},{96,128},{128,160},{160,192},{192,2... | collective-permute-start | bytes 884744 | tf_op jit(solution)/shard_map/while/body/eval_jaxpr/ppermute | solution.py:10
  222.1 14.6 %collective-permute-start = (bf16[1,1,384,384]{3,2,1,0:T(8,128)(2,1)S(1)}, bf16[1,1,384,384]{3,2,1,0:T(8,128)(2,1)S(1)}, u32[]{:S(2)}, u32[]{:S(2)}) collective-permute-start(bf16[1,1,384,384]{3,2,1,0:T(8,128)(2,1)S(1)} %get-tuple-element.124), channel_id=1, source_target_pairs={{480,0},{0,32},{32,64},{64,96},{96,128},{128,160},{160,192},{192,2... | collective-permute-start | bytes 884744 | tf_op jit(solution)/shard_map/while/body/eval_jaxpr/ppermute | solution.py:10
  236.9 14.6 %collective-permute-start = (bf16[1,1,384,384]{3,2,1,0:T(8,128)(2,1)S(1)}, bf16[1,1,384,384]{3,2,1,0:T(8,128)(2,1)S(1)}, u32[]{:S(2)}, u32[]{:S(2)}) collective-permute-start(bf16[1,1,384,384]{3,2,1,0:T(8,128)(2,1)S(1)} %get-tuple-element.124), channel_id=1, source_target_pairs={{480,0},{0,32},{32,64},{64,96},{96,128},{128,160},{160,192},{192,2... | collective-permute-start | bytes 884744 | tf_op jit(solution)/shard_map/while/body/eval_jaxpr/ppermute | solution.py:10
  251.7 14.6 %collective-permute-start = (bf16[1,1,384,384]{3,2,1,0:T(8,128)(2,1)S(1)}, bf16[1,1,384,384]{3,2,1,0:T(8,128)(2,1)S(1)}, u32[]{:S(2)}, u32[]{:S(2)}) collective-permute-start(bf16[1,1,384,384]{3,2,1,0:T(8,128)(2,1)S(1)} %get-tuple-element.124), channel_id=1, source_target_pairs={{480,0},{0,32},{32,64},{64,96},{96,128},{128,160},{160,192},{192,2... | collective-permute-start | bytes 884744 | tf_op jit(solution)/shard_map/while/body/eval_jaxpr/ppermute | solution.py:10
  271.8 5.0 %copy-start.1 = (bf16[1,16,384,384]{3,1,0,2:T(8,128)(2,1)S(1)}, bf16[1,16,384,384]{3,1,0,2:T(8,128)(2,1)}, u32[]{:S(2)}) copy-start(bf16[1,16,384,384]{3,1,0,2:T(8,128)(2,1)} %all-gather.2.cloned.1.call-done) | copy-start | bytes 14155780
  288.0 43.3 %copy-start.2 = (f32[32,32]{1,0:T(8,128)S(1)}, f32[32,32]{1,0:T(8,128)}, u32[]{:S(2)}) copy-start(f32[32,32]{1,0:T(8,128)} %param.14) | copy-start | bytes 12292
  294.5 52.6 %all-to-all-start = ((f32[1,32,8]{2,0,1:T(1,128)}), f32[1,32,8]{2,0,1:T(1,128)S(1)}, u32[]{:S(2)}, u32[]{:S(2)}) async-start(f32[1,32,8]{2,0,1:T(1,128)} %bitcast.11), calls=%async_computation | async-start | bytes 32768 | tf_op jit(solution)/shard_map/all_to_all | solution.py:58
  348.0 19.8 %all-to-all-start.1 = ((f32[2,32,8]{2,0,1:T(2,128)}), f32[2,32,8]{2,0,1:T(2,128)S(1)}, u32[]{:S(2)}, u32[]{:S(2)}) async-start(f32[2,32,8]{2,0,1:T(2,128)} %copy.31), calls=%async_computation.1 | async-start | bytes 65536 | tf_op jit(solution)/shard_map/all_to_all | solution.py:60
Sparse Core Ops, SparseCore 0:
  11.6 194.2 all-gather.1
where the time goes:
time: 477 us; the launch traced here: 470 us
  waiting for transfers between devices  245 us (51%)
  blocking collectives  94.2 us (20%)
  starting transfers between devices  80.1 us (17%)
  matrix products  17.2 us (4%)
  local copies, waits for them, and re-layouts  16.9 us (4%)
  between operations  14.2 us (3%)
    ppermute x15, waiting for transfers between devices, shifted(): return lax.ppermute(block, axis, route)  215 us
    unnamed x1, blocking collectives  94.2 us
    ppermute x15, starting transfers between devices, shifted(): return lax.ppermute(block, axis, route)  39.6 us
    all_to_all x1, starting transfers between devices, shards(): lax.all_to_all(entries, 'tau', split_axis=1, concat_axis=0, tiled=True)  36.7 us
    all_to_all x1, waiting for transfers between devices, shards(): lax.all_to_all(entries, 'tau', split_axis=1, concat_axis=0, tiled=True)  15.7 us
    all_to_all x1, waiting for transfers between devices, shards(): lax.all_to_all(freq_cols, 'tau', split_axis=1, concat_axis=2, tiled=True)  14.6 us
  transfers between devices with their start and end apart: 18, of which 17 were waited for; matrix products, arithmetic and copies ran while one was open for 1% of the time, Pallas kernels for 0%

commit v1 on v0

v1 whole, which is shorter than its diff:
```python
import functools

import jax
import jax.numpy as jnp
from jax import lax
from jax.experimental import pallas as pl
from jax.experimental.pallas import tpu as pltpu
from jax.sharding import Mesh
from jax.sharding import PartitionSpec as P

SIDE = 4
BLOCK = 16


def contract_kernel(b_ref, fwd_ref, back_t_ref, out_ref, left_ref, right_ref):
    blocks = b_ref.shape[0]
    orb = b_ref.shape[1]

    @pl.loop(0, blocks)
    def _(p):
        coef = b_ref[p]
        left = jnp.dot(coef, fwd_ref[...], preferred_element_type=jnp.float32)
        left_ref[p] = left.astype(jnp.bfloat16)
        right = jnp.dot(back_t_ref[...], coef, preferred_element_type=jnp.float32)
        right_ref[p] = right.astype(jnp.bfloat16)

    rows = blocks * BLOCK
    gram = jnp.zeros((rows, rows), jnp.float32)
    for at in range(0, orb, BLOCK):
        left = left_ref[:, at : at + BLOCK, :].reshape(rows, orb)
        right = right_ref[:, at : at + BLOCK, :].reshape(rows, orb)
        gram += lax.dot_general(
            left, right, (((1,), (1,)), ((), ())), preferred_element_type=jnp.float32
        )
    out_ref[...] = gram


def contract(coef, green_fwd, green_back_t):
    blocks, orb, _ = coef.shape
    rows = blocks * BLOCK
    gram = pl.pallas_call(
        contract_kernel,
        out_shape=jax.ShapeDtypeStruct((rows, rows), jnp.float32),
        in_specs=[pl.BlockSpec(memory_space=pltpu.VMEM)] * 3,
        out_specs=pl.BlockSpec(memory_space=pltpu.VMEM),
        scratch_shapes=[
            pltpu.VMEM((blocks, orb, orb), jnp.bfloat16),
            pltpu.VMEM((blocks, orb, orb), jnp.bfloat16),
        ],
        compiler_params=pltpu.CompilerParams(vmem_limit_bytes=40 * 1024 * 1024),
    )(coef, green_fwd, green_back_t)
    gram = gram.reshape(blocks, BLOCK, blocks, BLOCK)
    same = jnp.eye(BLOCK, dtype=jnp.float32)[None, :, None, :]
    return jnp.sum(gram * same, axis=(1, 3))


def spread(block, axes, count):
    copies = jnp.broadcast_to(block[None], (count,) + block.shape)
    return lax.all_to_all(copies, axes, 0, 0, tiled=True)


def shards(sizes, bcoef, fwd_green, back_green, kmq, ir_table, ir_fit, freq_index):
    zl, cores, ys, zh, xs = (sizes[name] for name in ("zl", "c", "y", "zh", "x"))
    blocks, rows, orb = bcoef.shape[1:]
    points = zl * cores
    minor = points // SIDE
    core = lax.axis_index("c")
    high = lax.axis_index("zh")
    low = lax.axis_index("zl")
    here_y, here_x = lax.axis_index("y"), lax.axis_index("x")

    own_k = low * cores + core
    target = kmq[0]
    major_shift = (own_k // minor - target // minor) % SIDE
    minor_shift = (own_k % minor - target % minor) % minor
    branch = (major_shift - 1) * (minor - 1) + minor_shift - 1

    transposed = [(c * zh + h, h * zh + c) for c in range(cores) for h in range(zh)]
    shard = lax.ppermute(bcoef.reshape(blocks * rows, orb), ("c", "zh"), transposed)
    green_fwd = lax.ppermute(fwd_green[0, 0], ("c", "zh"), transposed)

    def partner(major, minor_by):
        route = []
        for k in range(points):
            a, b = divmod(k, minor)
            source = (a - major) % SIDE * minor + (b - minor_by) % minor
            for h in range(zh):
                give = (source // cores * cores + source % cores) * zh + h
                take = (k // cores * cores + h) * zh + k % cores
                route.append((give, take))

        def move(block):
            return lax.ppermute(block, ("zl", "c", "zh"), route)

        return move

    moves = [partner(a, b) for a in range(1, SIDE) for b in range(1, minor)]
    green_back = lax.switch(branch, moves, back_green[0, 0])

    mine = spread(shard, ("y", "x"), ys * xs)
    other = lax.ppermute(mine, "c", [(0, 1), (1, 0)])
    first = jnp.where(core == 0, mine, other)
    second = jnp.where(core == 0, other, mine)
    both = jnp.stack([first, second]).reshape(cores, ys, xs, blocks, rows, orb)
    coef = both.transpose(3, 1, 0, 2, 4, 5).reshape(blocks, orb, orb)

    polar = contract(coef, green_fwd, green_back.T) * (-1.0 / points)

    pairs = polar.reshape(zl, 1, cores, blocks)
    pairs = jnp.broadcast_to(pairs, (zl, zh, cores, blocks)).reshape(zl * zh, cores, blocks)
    parts = lax.all_to_all(pairs, ("zl", "zh"), 0, 0, tiled=True)
    summed = jnp.sum(parts, axis=0)
    entries = jnp.broadcast_to(summed[:, None, :], (cores, ys * xs, blocks))
    entries = entries.reshape(cores * ys * xs, blocks)
    times = lax.all_to_all(entries, ("c", "y", "x"), 0, 0, tiled=True)

    own_w = (here_y * zh + high) * xs + here_x
    chosen = lax.dynamic_slice_in_dim(ir_table, freq_index[own_w], 1, axis=1)
    fit = ir_fit.reshape(-1, ys, cores, xs).transpose(0, 2, 1, 3).reshape(ir_fit.shape)
    transform = jnp.sum(chosen.transpose(0, 2, 1) * fit[None], axis=1)
    result = jnp.sum(transform[:, :, None] * times[None], axis=1)
    return result[:, None, None, :]


def solution(mesh):
    sizes = {"zl": 8, "c": 2, "y": 4, "zh": 2, "x": 4}
    fine = Mesh(mesh.devices.reshape(tuple(sizes.values())), tuple(sizes))
    ka, tau = ("zl", "c"), ("y", "zh", "x")
    return jax.shard_map(
        functools.partial(shards, sizes),
        mesh=fine,
        in_specs=(
            P(ka, None, tau, None),
            P(ka, tau, None, None),
            P(ka, tau, None, None),
            P(ka),
            P(),
            P(),
            P(),
        ),
        out_specs=P(None, tau, ka, None),
        check_vma=False,
    )
```

time: 477 us -> 167 us (0.35); the launches traced: 470 us -> 166 us
  waiting for transfers between devices: 245 us -> 43.9 us
  blocking collectives: 94.2 us -> 25.6 us
  starting transfers between devices: 80.1 us -> 55.2 us
  matrix products: 17.2 us -> 0 us
  between operations: 14.2 us -> 2.87 us
  Pallas kernels: 0 us -> 10.1 us
  other arithmetic: 1.78 us -> 10.5 us
    ppermute x15 -> x4, waiting for transfers between devices: 215 us -> 28.7 us  [the longest x1 25.6 us: move(): return lax.ppermute(block, ('zl', 'c', 'zh'), route)]
    unnamed x1 -> x0, blocking collectives: 94.2 us -> none
    all_to_all x0 -> x1, blocking collectives: none -> 25.6 us  [spread(): return lax.all_to_all(copies, axes, 0, 0, tiled=True)]
    all_to_all x2, starting transfers between devices: 40.5 us -> 20.7 us  [the longest x1 12.1 us: shards(): parts = lax.all_to_all(pairs, ('zl', 'zh'), 0, 0, tiled=True)]
    dot_general x6 -> x0, matrix products: 17.2 us -> none  [the longest x1 5.86 us: shards(): lax.dot_general(left_side.reshape(blocks, -1), right_side.reshape(blocks,...]
    all_to_all x2, waiting for transfers between devices: 30.3 us -> 15.2 us  [the longest x1 8.44 us: shards(): parts = lax.all_to_all(pairs, ('zl', 'zh'), 0, 0, tiled=True)]
    pallas_call x0 -> x1, Pallas kernels: none -> 10.1 us  [contract(): pl.pallas_call(contract_kernel, out_shape=jax.ShapeDtypeStruct((rows, row...]
    unnamed x11 -> x12, local copies, waits for them, and re-layouts: 8.56 us -> 1.05 us
  transfers between devices with their start and end apart: 18 -> 6, of which waited for: 17 -> 4; matrix products, arithmetic and copies ran while one was open for 1% -> 15% of each run, Pallas kernels for 0% -> 0%
where the time goes in v1:
time: 167 us; the launch traced here: 166 us
  starting transfers between devices  55.2 us (33%)
  waiting for transfers between devices  43.9 us (26%)
  blocking collectives  25.6 us (15%)
  local copies, waits for them, and re-layouts  18.2 us (11%)
  other arithmetic  10.5 us (6%)
  Pallas kernels  10.1 us (6%)
  between operations  2.87 us (2%)
    all_to_all x1, blocking collectives, spread(): return lax.all_to_all(copies, axes, 0, 0, tiled=True)  25.6 us
    ppermute x1, waiting for transfers between devices, move(): return lax.ppermute(block, ('zl', 'c', 'zh'), route)  25.6 us
    ppermute x1, starting transfers between devices, shards(): lax.ppermute(bcoef.reshape(blocks * rows, orb), ('c', 'zh'), transposed)  16.8 us
    ppermute x1, starting transfers between devices, shards(): green_fwd = lax.ppermute(fwd_green[0, 0], ('c', 'zh'), transposed)  13.8 us
    all_to_all x1, starting transfers between devices, shards(): parts = lax.all_to_all(pairs, ('zl', 'zh'), 0, 0, tiled=True)  12.1 us
    pallas_call x1, Pallas kernels, contract(): pl.pallas_call(contract_kernel, out_shape=jax.ShapeDtypeStruct((rows, row...  10.1 us
    all_to_all x1, starting transfers between devices, shards(): times = lax.all_to_all(entries, ('c', 'y', 'x'), 0, 0, tiled=True)  8.65 us
    all_to_all x1, waiting for transfers between devices, shards(): parts = lax.all_to_all(pairs, ('zl', 'zh'), 0, 0, tiled=True)  8.44 us
  transfers between devices with their start and end apart: 6, of which 4 were waited for; matrix products, arithmetic and copies ran while one was open for 15% of the time, Pallas kernels for 0%

profile of v1, /device:TPU:1, one launch (start us, length us, event | category | flops | bytes accessed | tf_op | source)
XLA Modules:
  0.0 166.4 jit_solution(6856859033818132315)
XLA Ops:
  0.0 0.9 copy.54
  1.0 16.8 %collective-permute-start.9 = (bf16[192,384]{1,0:T(8,128)(2,1)S(1)}, bf16[192,384]{1,0:T(8,128)(2,1)S(1)}, u32[]{:S(2)}, u32[]{:S(2)}) collective-permute-start(bf16[192,384]{1,0:T(8,128)(2,1)S(1)} %reshape.48), channel_id=1, source_target_pairs={{0,0},{4,32},{32,4},{36,36},{1,1},{5,33},{33,5},{37,37},{2,2},{6,3... | collective-permute-start | bytes 442376 | tf_op jit(solution)/shard_map/ppermute | solution.py:79
  17.8 3.1 %collective-permute-done.9 = bf16[192,384]{1,0:T(8,128)(2,1)S(1)} collective-permute-done((bf16[192,384]{1,0:T(8,128)(2,1)S(1)}, bf16[192,384]{1,0:T(8,128)(2,1)S(1)}, u32[]{:S(2)}, u32[]{:S(2)}) %collective-permute-start.9) | collective-permute-done | bytes 147488 | tf_op jit(solution)/shard_map/ppermute | solution.py:79
  21.0 0.3 broadcast_in_dim.8
  21.3 25.6 %all_to_all.19 = bf16[16,192,384]{2,1,0:T(8,128)(2,1)S(1)} all-to-all(bf16[16,192,384]{2,1,0:T(8,128)(2,1)S(1)} %broadcast_in_dim.8), channel_id=1, replica_groups=mesh['zl'=8,'c'=2,'y'=4,'zh'=2,'x'=4] {'y','x'}, dimensions={0} | all-to-all | bytes 4718592 | tf_op jit(solution)/shard_map/all_to_all | solution.py:59
  46.9 1.9 %collective-permute-start.10 = (bf16[16,192,384]{2,1,0:T(8,128)(2,1)S(1)}, bf16[16,192,384]{2,1,0:T(8,128)(2,1)}, u32[]{:S(2)}, u32[]{:S(2)}) collective-permute-start(bf16[16,192,384]{2,1,0:T(8,128)(2,1)S(1)} %all_to_all.19), channel_id=1, source_target_pairs={{0,32},{32,0},{1,33},{33,1},{2,34},{34,2},{3,35},{35,3},{4,36},{36... | collective-permute-start | bytes 7077896 | tf_op jit(solution)/shard_map/ppermute | solution.py:101
  48.9 13.8 %collective-permute-start.11 = (bf16[384,384]{1,0:T(8,128)(2,1)S(1)}, bf16[384,384]{1,0:T(8,128)(2,1)S(1)}, u32[]{:S(2)}, u32[]{:S(2)}) collective-permute-start(bf16[384,384]{1,0:T(8,128)(2,1)S(1)} %bitcast.42), channel_id=1, source_target_pairs={{0,0},{4,32},{32,4},{36,36},{1,1},{5,33},{33,5},{37,37},{2,2},{6,3... | collective-permute-start | bytes 884744 | tf_op jit(solution)/shard_map/ppermute | solution.py:80
  63.4 27.5 %conditional.1 = (bf16[384,384]{1,0:T(8,128)(2,1)}) conditional(s32[]{:T(128)} %clamp.3, bf16[384,384]{1,0:T(8,128)(2,1)S(1)} %bitcast.33, bf16[384,384]{1,0:T(8,128)(2,1)S(1)} %bitcast.34, bf16[384,384]{1,0:T(8,128)(2,1)S(1)} %bitcast.35, bf16[384,384]{1,0:T(8,128)(2,1)S(1)} %bitcast.36, ...), branch_computations={%region_1.2_spmd, %region_2.3_spmd, %region_3.4_spmd, %region_4.5_... | conditional | bytes 1179696 | solution.py:98
  63.4 1.9 %collective-permute-start.7 = (bf16[384,384]{1,0:T(8,128)(2,1)S(1)}, bf16[384,384]{1,0:T(8,128)(2,1)}, u32[]{:S(2)}, u32[]{:S(2)}) collective-permute-start(bf16[384,384]{1,0:T(8,128)(2,1)S(1)} %param.7), channel_id=1, source_target_pairs={{192,0},{196,32},{224,4},{228,36},{128,64},{132,96},{160,68},{164,... | collective-permute-start | bytes 884744 | tf_op jit(solution)/shard_map/cond/branch_7_fun/ppermute | solution.py:93
  65.4 25.6 %collective-permute-done.7 = bf16[384,384]{1,0:T(8,128)(2,1)} collective-permute-done((bf16[384,384]{1,0:T(8,128)(2,1)S(1)}, bf16[384,384]{1,0:T(8,128)(2,1)}, u32[]{:S(2)}, u32[]{:S(2)}) %collective-permute-start.7) | collective-permute-done | bytes 294944 | tf_op jit(solution)/shard_map/cond/branch_7_fun/ppermute | solution.py:93
  91.0 1.2 copy.58
  92.1 3.5 %broadcast_select_fusion.1 = (bf16[16,192,384]{2,1,0:T(8,128)(2,1)}, bf16[16,192,384]{2,1,0:T(8,128)(2,1)S(1)}) fusion(bf16[16,192,384]{2,1,0:T(8,128)(2,1)S(1)} %all_to_all.19, bf16[16,192,384]{2,1,0:T(8,128)(2,1)} %collective-permute-done.10, pred[]{:T(512)S(6)} %eq.16), kind=kLoop, calls=%fused_computation.2 | loop fusion | flops 2359296 | bytes 9437185 | tf_op jit(solution)/shard_map/jit(_where)/select_n | solution.py:102
  95.7 1.4 copy.56
  97.1 2.3 %stack.10 = bf16[1,4,4,16,12,384]{5,2,1,4,3,0:T(4,128)(2,1)} reshape(bf16[16,192,384]{2,0,1:T(8,128)(2,1)S(1)} %copy.56) | data formatting | bytes 4718592 | tf_op jit(solution)/shard_map/stack | solution.py:104
  99.4 3.0 %copy.55 = bf16[16,192,384]{2,0,1:T(8,128)(2,1)S(1)} copy(bf16[16,192,384]{2,1,0:T(8,128)(2,1)} %get-tuple-element.24) | data formatting | bytes 4718592 | tf_op jit(solution)/shard_map/jit(_where)/select_n | solution.py:102
  102.4 2.2 %stack.9 = bf16[1,4,4,16,12,384]{5,2,1,4,3,0:T(4,128)(2,1)} reshape(bf16[16,192,384]{2,0,1:T(8,128)(2,1)S(1)} %copy.55) | data formatting | bytes 4718592 | tf_op jit(solution)/shard_map/stack | solution.py:104
  104.6 5.9 %maximum_bitcast_fusion = bf16[16,4,2,4,12,384]{5,3,1,4,0,2:T(4,128)(2,1)S(1)} fusion(bf16[1,4,4,16,12,384]{5,2,1,4,3,0:T(4,128)(2,1)} %stack.10, bf16[1,4,4,16,12,384]{5,2,1,4,3,0:T(4,128)(2,1)} %stack.9), kind=kLoop, calls=%fused_computation | loop fusion | flops 2359296 | bytes 9437184 | tf_op jit(solution)/shard_map/transpose | solution.py:105
  110.5 2.8 %copy.57 = bf16[16,4,2,4,12,384]{5,0,4,3,2,1:T(8,128)(2,1)S(1)} copy(bf16[16,4,2,4,12,384]{5,3,1,4,0,2:T(4,128)(2,1)S(1)} %maximum_bitcast_fusion) | data formatting | bytes 9437184 | tf_op jit(solution)/shard_map/transpose | solution.py:105
  113.3 1.1 copy.59.b_ref
  114.5 10.1 %shard_map.73 = f32[256,256]{1,0:T(8,128)S(1)} custom-call(bf16[16,384,384]{2,1,0:T(8,128)(2,1)S(1)} %copy.59.b_ref, bf16[384,384]{1,0:T(8,128)(2,1)S(1)} %collective-permute-done.11.fwd_ref, bf16[384,384]{1,0:T(8,128)(2,1)S(1)} %bitcast.27), custom_call_target="tpu_custom_call" | custom-call | tf_op jit(solution)/shard_map/pallas_call | solution.py:41
  124.6 0.6 reshape.50
  125.3 0.3 multiply_reduce_fusion
  125.6 0.6 broadcast_in_dim.9
  126.2 12.1 %all-to-all-start.1 = ((f32[16,2,16]{2,1,0:T(2,128)}), f32[16,2,16]{2,1,0:T(2,128)S(1)}, u32[]{:S(2)}, u32[]{:S(2)}) async-start(f32[16,2,16]{2,1,0:T(2,128)} %bitcast.11), calls=%async_computation.1 | async-start | bytes 32768 | tf_op jit(solution)/shard_map/all_to_all | solution.py:111
  138.4 0.6 dynamic_slice.6
  141.0 0.2 dynamic-slice_reduce_fusion
  141.1 8.4 %all-to-all-done.1 = f32[16,2,16]{2,1,0:T(2,128)S(1)} async-done(((f32[16,2,16]{2,1,0:T(2,128)}), f32[16,2,16]{2,1,0:T(2,128)S(1)}, u32[]{:S(2)}, u32[]{:S(2)}) %all-to-all-start.1) | async-done | bytes 2080 | tf_op jit(solution)/shard_map/all_to_all | solution.py:111
  149.6 0.6 broadcast_in_dim.10
  150.2 8.7 %all-to-all-start.2 = ((f32[32,1,16]{2,1,0:T(1,128)}), f32[32,1,16]{2,1,0:T(1,128)S(1)}, u32[]{:S(2)}, u32[]{:S(2)}) async-start(f32[32,1,16]{2,1,0:T(1,128)} %bitcast.12), calls=%async_computation.2 | async-start | bytes 32768 | tf_op jit(solution)/shard_map/all_to_all | solution.py:115
  158.9 0.1 multiply_reduce_fusion.1
  158.9 6.7 %all-to-all-done.2 = f32[32,1,16]{2,1,0:T(1,128)S(1)} async-done(((f32[32,1,16]{2,1,0:T(1,128)}), f32[32,1,16]{2,1,0:T(1,128)S(1)}, u32[]{:S(2)}, u32[]{:S(2)}) %all-to-all-start.2) | async-done | bytes 2080 | tf_op jit(solution)/shard_map/all_to_all | solution.py:115
  165.7 0.7 multiply_reduce_fusion.2
  (20 shorter events, 0.3 us)
Async XLA Ops:
  0.0 141.0 %copy-start = (f32[2,128,32]{1,2,0:T(8,128)S(1)}, f32[2,128,32]{1,2,0:T(8,128)}, u32[]{:S(2)}) copy-start(f32[2,128,32]{1,2,0:T(8,128)} %param.20) | copy-start | bytes 98308
  1.0 20.0 %collective-permute-start.9 = (bf16[192,384]{1,0:T(8,128)(2,1)S(1)}, bf16[192,384]{1,0:T(8,128)(2,1)S(1)}, u32[]{:S(2)}, u32[]{:S(2)}) collective-permute-start(bf16[192,384]{1,0:T(8,128)(2,1)S(1)} %reshape.48), channel_id=1, source_target_pairs={{0,0},{4,32},{32,4},{36,36},{1,1},{5,33},{33,5},{37,37},{2,2},{6,3... | collective-permute-start | bytes 442376 | tf_op jit(solution)/shard_map/ppermute | solution.py:79
  21.3 27.6 %copy-start.3 = (bf16[1,1,384,384]{3,2,1,0:T(8,128)(2,1)S(1)}, bf16[1,1,384,384]{3,2,1,0:T(8,128)(2,1)}, u32[]{:S(2)}) copy-start(bf16[1,1,384,384]{3,2,1,0:T(8,128)(2,1)} %param.17) | copy-start | bytes 884740
  21.3 42.1 %copy-start.2 = (bf16[1,1,384,384]{3,2,1,0:T(8,128)(2,1)S(1)}, bf16[1,1,384,384]{3,2,1,0:T(8,128)(2,1)}, u32[]{:S(2)}) copy-start(bf16[1,1,384,384]{3,2,1,0:T(8,128)(2,1)} %param.18) | copy-start | bytes 884740
  46.9 45.2 %collective-permute-start.10 = (bf16[16,192,384]{2,1,0:T(8,128)(2,1)S(1)}, bf16[16,192,384]{2,1,0:T(8,128)(2,1)}, u32[]{:S(2)}, u32[]{:S(2)}) collective-permute-start(bf16[16,192,384]{2,1,0:T(8,128)(2,1)S(1)} %all_to_all.19), channel_id=1, source_target_pairs={{0,32},{32,0},{1,33},{33,1},{2,34},{34,2},{3,35},{35,3},{4,36},{36... | collective-permute-start | bytes 7077896 | tf_op jit(solution)/shard_map/ppermute | solution.py:101
  48.9 65.6 %collective-permute-start.11 = (bf16[384,384]{1,0:T(8,128)(2,1)S(1)}, bf16[384,384]{1,0:T(8,128)(2,1)S(1)}, u32[]{:S(2)}, u32[]{:S(2)}) collective-permute-start(bf16[384,384]{1,0:T(8,128)(2,1)S(1)} %bitcast.42), channel_id=1, source_target_pairs={{0,0},{4,32},{32,4},{36,36},{1,1},{5,33},{33,5},{37,37},{2,2},{6,3... | collective-permute-start | bytes 884744 | tf_op jit(solution)/shard_map/ppermute | solution.py:80
  63.4 27.5 %collective-permute-start.7 = (bf16[384,384]{1,0:T(8,128)(2,1)S(1)}, bf16[384,384]{1,0:T(8,128)(2,1)}, u32[]{:S(2)}, u32[]{:S(2)}) collective-permute-start(bf16[384,384]{1,0:T(8,128)(2,1)S(1)} %param.7), channel_id=1, source_target_pairs={{192,0},{196,32},{224,4},{228,36},{128,64},{132,96},{160,68},{164,... | collective-permute-start | bytes 884744 | tf_op jit(solution)/shard_map/cond/branch_7_fun/ppermute | solution.py:93
  124.6 13.6 %copy-start.1 = (f32[32,32]{1,0:T(8,128)S(1)}, f32[32,32]{1,0:T(8,128)}, u32[]{:S(2)}) copy-start(f32[32,32]{1,0:T(8,128)} %param.21) | copy-start | bytes 12292
  124.6 13.8 %copy-start.4 = (s32[32]{0:T(128)S(1)}, s32[32]{0:T(128)}, u32[]{:S(2)}) copy-start(s32[32]{0:T(128)} %param.22) | copy-start | bytes 388
  126.2 23.4 %all-to-all-start.1 = ((f32[16,2,16]{2,1,0:T(2,128)}), f32[16,2,16]{2,1,0:T(2,128)S(1)}, u32[]{:S(2)}, u32[]{:S(2)}) async-start(f32[16,2,16]{2,1,0:T(2,128)} %bitcast.11), calls=%async_computation.1 | async-start | bytes 32768 | tf_op jit(solution)/shard_map/all_to_all | solution.py:111
  150.2 15.5 %all-to-all-start.2 = ((f32[32,1,16]{2,1,0:T(1,128)}), f32[32,1,16]{2,1,0:T(1,128)S(1)}, u32[]{:S(2)}, u32[]{:S(2)}) async-start(f32[32,1,16]{2,1,0:T(1,128)} %bitcast.12), calls=%async_computation.2 | async-start | bytes 32768 | tf_op jit(solution)/shard_map/all_to_all | solution.py:115

commit v2 on v1

v2 whole, which is shorter than its diff:
```python
import functools

import jax
import jax.numpy as jnp
from jax import lax
from jax.experimental import pallas as pl
from jax.experimental.pallas import tpu as pltpu
from jax.sharding import Mesh
from jax.sharding import PartitionSpec as P

SIDE = 4
TILE = 16
VMEM_LIMIT = 24 * 1024 * 1024


def onehot(rows, columns):
    return (rows == columns).astype(jnp.float32).astype(jnp.bfloat16)


def swap_order(blocks):
    size = TILE * blocks
    at = lax.broadcasted_iota(jnp.int32, (size, size), 0)
    source = lax.broadcasted_iota(jnp.int32, (size, size), 1)
    return onehot(at % TILE * blocks + at // TILE, source)


def ordered(order, piece_ref, group, blocks):
    size = TILE * blocks
    piece = piece_ref[pl.ds(pl.multiple_of(group * size, size), size), :]
    return jnp.dot(order, piece, preferred_element_type=jnp.float32).astype(jnp.bfloat16)


def left_kernel(mine_ref, fwd_ref, coef_ref, left_ref):
    blocks = coef_ref.shape[0]
    width = fwd_ref.shape[-1]
    order = swap_order(blocks)

    @pl.loop(0, coef_ref.shape[1] // TILE)
    def _(group):
        coef = ordered(order, mine_ref, group, blocks)
        left = jnp.dot(coef, fwd_ref[...], preferred_element_type=jnp.float32)
        spot = pl.ds(pl.multiple_of(group * TILE, TILE), TILE)
        coef_ref[:, spot, :] = coef.reshape(blocks, TILE, width)
        left_ref[:, spot, :] = left.astype(jnp.bfloat16).reshape(blocks, TILE, width)


def product_kernel(
    core_ref, coef_mine_ref, left_mine_ref, other_ref, fwd_ref, back_ref, out_ref, coef_ref, left_ref, back_t_ref, right_ref
):
    blocks, half, width = coef_mine_ref.shape
    core = core_ref[0]
    order = swap_order(blocks)
    run = 3 * TILE

    @pl.loop(0, half // TILE)
    def _(group):
        coef = ordered(order, other_ref, group, blocks)
        left = jnp.dot(coef, fwd_ref[...], preferred_element_type=jnp.float32)
        spot = pl.ds(pl.multiple_of(group * TILE, TILE), TILE)
        coef_ref[:, spot, :] = coef.reshape(blocks, TILE, width)
        left_ref[:, spot, :] = left.astype(jnp.bfloat16).reshape(blocks, TILE, width)

    def picked(side):
        starts = [pl.multiple_of(y * 2 * run + side * run, TILE) for y in range(SIDE)]
        return jnp.concatenate([back_ref[pl.ds(at, run), :] for at in starts], axis=0)

    back_t_ref[0] = picked(core).T
    back_t_ref[1] = picked(1 - core).T

    @pl.loop(0, blocks)
    def _(p):
        right = jnp.dot(back_t_ref[0], coef_mine_ref[p], preferred_element_type=jnp.float32)
        right += jnp.dot(back_t_ref[1], coef_ref[p], preferred_element_type=jnp.float32)
        right_ref[p] = right.astype(jnp.bfloat16)

    size = TILE * blocks
    gram = jnp.zeros((size, size), jnp.float32)
    for side, lefts in ((core, left_mine_ref), (1 - core, left_ref)):
        for y in range(SIDE):
            for part in range(run // TILE):
                at = y * run + part * TILE
                natural = pl.multiple_of(y * 2 * run + side * run + part * TILE, TILE)
                left = lefts[:, at : at + TILE, :].reshape(size, width)
                right = right_ref[:, pl.ds(natural, TILE), :].reshape(size, width)
                gram += lax.dot_general(
                    left, right, (((1,), (1,)), ((), ())), preferred_element_type=jnp.float32
                )
    row = lax.broadcasted_iota(jnp.int32, (size, size), 0) % TILE
    column = lax.broadcasted_iota(jnp.int32, (size, size), 1) % TILE
    gram = jnp.where(row == column, gram, 0.0)
    gram = jnp.sum(gram.reshape(blocks, TILE, size), axis=1)
    at = lax.broadcasted_iota(jnp.int32, (size, blocks), 0) // TILE
    which = lax.broadcasted_iota(jnp.int32, (size, blocks), 1)
    pick = (at == which).astype(jnp.float32)
    out_ref[...] = jnp.dot(
        gram, pick, precision=lax.Precision.HIGHEST, preferred_element_type=jnp.float32
    )


def left_half(mine, green_fwd, blocks):
    width = green_fwd.shape[-1]
    shape = jax.ShapeDtypeStruct((blocks, mine.shape[0] // blocks, width), jnp.bfloat16)
    return pl.pallas_call(
        left_kernel,
        out_shape=(shape, shape),
        in_specs=[pl.BlockSpec(memory_space=pltpu.VMEM)] * 2,
        out_specs=[pl.BlockSpec(memory_space=pltpu.VMEM)] * 2,
        compiler_params=pltpu.CompilerParams(vmem_limit_bytes=VMEM_LIMIT),
        cost_estimate=pl.CostEstimate(
            flops=2_000_000_000, bytes_accessed=7_000_000, transcendentals=0
        ),
    )(mine, green_fwd)


def product(core, coef_mine, left_mine, other, green_fwd, green_back):
    blocks, half, width = coef_mine.shape
    return pl.pallas_call(
        product_kernel,
        out_shape=jax.ShapeDtypeStruct((blocks, blocks), jnp.float32),
        in_specs=[pl.BlockSpec(memory_space=pltpu.SMEM)]
        + [pl.BlockSpec(memory_space=pltpu.VMEM)] * 5,
        out_specs=pl.BlockSpec(memory_space=pltpu.VMEM),
        scratch_shapes=[
            pltpu.VMEM((blocks, half, width), jnp.bfloat16),
            pltpu.VMEM((blocks, half, width), jnp.bfloat16),
            pltpu.VMEM((2, width, half), jnp.bfloat16),
            pltpu.VMEM((blocks, width, width), jnp.bfloat16),
        ],
        compiler_params=pltpu.CompilerParams(vmem_limit_bytes=VMEM_LIMIT),
        cost_estimate=pl.CostEstimate(
            flops=5_000_000_000, bytes_accessed=10_000_000, transcendentals=0
        ),
    )(core, coef_mine, left_mine, other, green_fwd, green_back)


def spread(block, axes, count):
    copies = jnp.broadcast_to(block[None], (count,) + block.shape)
    return lax.all_to_all(copies, axes, 0, 0, tiled=True)


def shards(sizes, bcoef, fwd_green, back_green, kmq, ir_table, ir_fit, freq_index):
    zl, cores, ys, zh, xs = (sizes[name] for name in ("zl", "c", "y", "zh", "x"))
    blocks, rows, orb = bcoef.shape[1:]
    points = zl * cores
    minor = points // SIDE
    core = lax.axis_index("c")
    high = lax.axis_index("zh")
    low = lax.axis_index("zl")
    here_y, here_x = lax.axis_index("y"), lax.axis_index("x")

    own_k = low * cores + core
    target = kmq[0]
    major_shift = ((own_k >> 2) - (target >> 2)) & 3
    minor_shift = ((own_k & 3) - (target & 3)) & 3
    branch = (major_shift - 1) * (minor - 1) + minor_shift - 1

    transposed = [(c * zh + h, h * zh + c) for c in range(cores) for h in range(zh)]

    def partner(major, minor_by):
        route = []
        for k in range(points):
            a, b = divmod(k, minor)
            source = (a - major) % SIDE * minor + (b - minor_by) % minor
            for h in range(zh):
                route.append((source * zh + h, (k // cores * cores + h) * zh + k % cores))

        def work(shard, green_fwd, green_back):
            shard = shard.transpose(1, 0, 2).reshape(rows * blocks, orb)
            shard = lax.ppermute(shard, ("c", "zh"), transposed)
            green_fwd = lax.ppermute(green_fwd, ("c", "zh"), transposed)
            green_back = lax.ppermute(green_back, ("zl", "c", "zh"), route)
            mine = spread(shard, ("y", "x"), ys * xs).reshape(ys * xs * rows * blocks, orb)
            mine, green_fwd, green_back = lax.optimization_barrier((mine, green_fwd, green_back))
            other = lax.ppermute(mine, "c", [(0, 1), (1, 0)])
            coef_mine, left_mine = left_half(mine, green_fwd, blocks)
            return product(core[None], coef_mine, left_mine, other, green_fwd, green_back)

        return work

    works = [partner(a, b) for a in range(1, SIDE) for b in range(1, minor)]
    polar = lax.switch(branch, works, bcoef[0], fwd_green[0, 0], back_green[0, 0])
    polar = polar * (-1.0 / points)

    pairs = polar.reshape(zl, 1, cores, blocks)
    pairs = jnp.broadcast_to(pairs, (zl, zh, cores, blocks)).reshape(zl * zh, cores, blocks)
    parts = lax.all_to_all(pairs, ("zl", "zh"), 0, 0, tiled=True)
    summed = jnp.sum(parts, axis=0)
    entries = jnp.broadcast_to(summed[:, None, :], (cores, ys * xs, blocks))
    entries = entries.reshape(cores * ys * xs, blocks)
    times = lax.all_to_all(entries, ("c", "y", "x"), 0, 0, tiled=True)

    own_w = (here_y * zh + high) * xs + here_x
    chosen = lax.dynamic_slice_in_dim(ir_table, freq_index[own_w], 1, axis=1)
    fit = ir_fit.reshape(-1, ys, cores, xs).transpose(0, 2, 1, 3).reshape(ir_fit.shape)
    transform = jnp.sum(chosen.transpose(0, 2, 1) * fit[None], axis=1)
    result = jnp.sum(transform[:, :, None] * times[None], axis=1)
    return result[:, None, None, :]


def solution(mesh):
    sizes = {"zl": 8, "c": 2, "y": 4, "zh": 2, "x": 4}
    fine = Mesh(mesh.devices.reshape(tuple(sizes.values())), tuple(sizes))
    ka, tau = ("zl", "c"), ("y", "zh", "x")
    return jax.shard_map(
        functools.partial(shards, sizes),
        mesh=fine,
        in_specs=(
            P(ka, None, tau, None),
            P(ka, tau, None, None),
            P(ka, tau, None, None),
            P(ka),
            P(),
            P(),
            P(),
        ),
        out_specs=P(None, tau, ka, None),
        check_vma=False,
    )
```

time: 167 us -> 137 us (0.82)
  blocking collectives: 25.6 us -> 0 us
  local copies, waits for them, and re-layouts: 18.2 us -> 3.89 us
  other arithmetic: 10.5 us -> 0.78 us
  starting transfers between devices: 55.2 us -> 64.1 us
  Pallas kernels: 10.1 us -> 18.6 us
  waiting for transfers between devices: 43.9 us -> 46.2 us
    all_to_all x1 -> x0, blocking collectives: 25.6 us -> none  [spread(): return lax.all_to_all(copies, axes, 0, 0, tiled=True)]
    pallas_call x1 -> x2, Pallas kernels: 10.1 us -> 18.6 us  [the longest x1 13.3 us: product(): pl.pallas_call(product_kernel, out_shape=jax.ShapeDtypeStruct((blocks, bl...]
    all_to_all x0 -> x1, starting transfers between devices: none -> 6.89 us  [spread(): return lax.all_to_all(copies, axes, 0, 0, tiled=True)]
    transpose x1 -> x0, other arithmetic: 5.91 us -> none  [shards(): coef = both.transpose(3, 1, 0, 2, 4, 5).reshape(blocks, orb, orb)]
    another operation x2 -> x0, local copies, waits for them, and re-layouts: 4.5 us -> none  [shards(): both = jnp.stack([first, second]).reshape(cores, ys, xs, blocks, rows, orb)]
    select_n x2 -> x0, local copies, waits for them, and re-layouts: 4.44 us -> none  [the longest x1 3.05 us: shards(): first = jnp.where(core == 0, mine, other)]
    select_n x1 -> x0, other arithmetic: 3.52 us -> none  [shards(): first = jnp.where(core == 0, mine, other)]
    all_to_all x1, starting transfers between devices: 12.1 us -> 15 us  [shards(): parts = lax.all_to_all(pairs, ('zl', 'zh'), 0, 0, tiled=True)]
  transfers between devices with their start and end apart: 6 -> 7, of which waited for: 4 -> 5; matrix products, arithmetic and copies ran while one was open for 15% -> 1% of each run, Pallas kernels for 0% -> 4%
where the time goes in v2:
time: 137 us
  starting transfers between devices  64.1 us (47%)
  waiting for transfers between devices  46.2 us (34%)
  Pallas kernels  18.6 us (14%)
  local copies, waits for them, and re-layouts  3.89 us (3%)
  between operations  2.71 us (2%)
    ppermute x1, waiting for transfers between devices, work(): green_back = lax.ppermute(green_back, ('zl', 'c', 'zh'), route)  25.1 us
    ppermute x1, starting transfers between devices, work(): shard = lax.ppermute(shard, ('c', 'zh'), transposed)  16.8 us
    all_to_all x1, starting transfers between devices, shards(): parts = lax.all_to_all(pairs, ('zl', 'zh'), 0, 0, tiled=True)  15 us
    pallas_call x1, Pallas kernels, product(): pl.pallas_call(product_kernel, out_shape=jax.ShapeDtypeStruct((blocks, bl...  13.3 us
    ppermute x1, starting transfers between devices, work(): green_fwd = lax.ppermute(green_fwd, ('c', 'zh'), transposed)  12.7 us
    all_to_all x1, starting transfers between devices, shards(): times = lax.all_to_all(entries, ('c', 'y', 'x'), 0, 0, tiled=True)  8.85 us
    all_to_all x1, waiting for transfers between devices, shards(): parts = lax.all_to_all(pairs, ('zl', 'zh'), 0, 0, tiled=True)  8.42 us
    all_to_all x1, starting transfers between devices, spread(): return lax.all_to_all(copies, axes, 0, 0, tiled=True)  6.89 us
  transfers between devices with their start and end apart: 7, of which 5 were waited for; matrix products, arithmetic and copies ran while one was open for 1% of the time, Pallas kernels for 4%

profile of v2, /device:TPU:1, one launch (start us, length us, event | category | flops | bytes accessed | tf_op | source)
XLA Modules:
  0.0 136.8 jit_solution(13250703583594138564)
XLA Ops:
  0.0 0.0 copy-start
  0.7 0.0 copy-start.11
  0.7 0.0 copy-start.1
  0.7 92.2 %conditional.1 = (f32[16,16]{1,0:T(8,128)S(1)}) conditional(s32[]{:T(128)} %clamp.3, (s32[]{:T(128)}, bf16[16,12,384]{2,0,1:T(8,128)(2,1)}, bf16[384,384]{1,0:T(8,128)(2,1)}, bf16[384,384]{1,0:T(8,128)(2,1)}) %tuple.69, (s32[]{:T(128)}, bf16[16,12,384]{2,0,1:T(8,128)(2,1)}, bf16[384,384]{1,0:T(8,128)(2,1)}, ...), branch_computations={%region_1.0_spmd, %region_2.0_spmd, %region_3.0_spmd, %region_4.0_... | conditional | flops 7000000000 | bytes 40150820 | solution.py:181
  0.9 16.8 %collective-permute-start.24 = (bf16[192,384]{1,0:T(8,128)(2,1)}, bf16[192,384]{1,0:T(8,128)(2,1)S(1)}, u32[]{:S(2)}, u32[]{:S(2)}) collective-permute-start(bf16[192,384]{1,0:T(8,128)(2,1)} %bitcast.117), channel_id=1, source_target_pairs={{0,0},{4,32},{32,4},{36,36},{1,1},{5,33},{33,5},{37,37},{2,2},{6,3... | collective-permute-start | bytes 442376 | tf_op jit(solution)/shard_map/cond/branch_6_fun/ppermute | solution.py:169
  17.7 3.3 %collective-permute-done.24 = bf16[192,384]{1,0:T(8,128)(2,1)S(1)} collective-permute-done((bf16[192,384]{1,0:T(8,128)(2,1)}, bf16[192,384]{1,0:T(8,128)(2,1)S(1)}, u32[]{:S(2)}, u32[]{:S(2)}) %collective-permute-start.24) | collective-permute-done | bytes 147488 | tf_op jit(solution)/shard_map/cond/branch_6_fun/ppermute | solution.py:169
  21.1 1.7 %broadcast_in_dim.70 = bf16[16,192,384]{2,1,0:T(8,128)(2,1)} broadcast(bf16[192,384]{1,0:T(8,128)(2,1)S(1)} %collective-permute-done.24), dimensions={1,2} | broadcast | bytes 2506752 | tf_op jit(solution)/shard_map/cond/branch_6_fun/broadcast_in_dim | solution.py:137
  22.8 6.9 %all-to-all-start.6 = ((bf16[16,192,384]{2,1,0:T(8,128)(2,1)}), bf16[16,192,384]{2,1,0:T(8,128)(2,1)S(1)}, u32[]{:S(2)}, u32[]{:S(2)}) async-start(bf16[16,192,384]{2,1,0:T(8,128)(2,1)} %broadcast_in_dim.70), calls=%async_computation.6 | async-start | bytes 4718592 | tf_op jit(solution)/shard_map/cond/branch_6_fun/all_to_all | solution.py:138
  29.7 0.0 copy-done.8
  29.7 12.7 %collective-permute-start.25 = (bf16[384,384]{1,0:T(8,128)(2,1)S(1)}, bf16[384,384]{1,0:T(8,128)(2,1)S(1)}, u32[]{:S(2)}, u32[]{:S(2)}) collective-permute-start(bf16[384,384]{1,0:T(8,128)(2,1)S(1)} %copy-done.8), channel_id=1, source_target_pairs={{0,0},{4,32},{32,4},{36,36},{1,1},{5,33},{33,5},{37,37},{2,2},{6,3... | collective-permute-start | bytes 884744 | tf_op jit(solution)/shard_map/cond/branch_6_fun/ppermute | solution.py:170
  42.3 1.9 %collective-permute-start.26 = (bf16[384,384]{1,0:T(8,128)(2,1)}, bf16[384,384]{1,0:T(8,128)(2,1)S(1)}, u32[]{:S(2)}, u32[]{:S(2)}) collective-permute-start(bf16[384,384]{1,0:T(8,128)(2,1)} %get-tuple-element.144), channel_id=1, source_target_pairs={{224,0},{228,32},{128,4},{132,36},{160,64},{164,96},{192,68},{196,... | collective-permute-start | bytes 884744 | tf_op jit(solution)/shard_map/cond/branch_6_fun/ppermute | solution.py:171
  44.3 2.8 %collective-permute-done.25.fwd_ref = bf16[384,384]{1,0:T(8,128)(2,1)S(1)} collective-permute-done((bf16[384,384]{1,0:T(8,128)(2,1)S(1)}, bf16[384,384]{1,0:T(8,128)(2,1)S(1)}, u32[]{:S(2)}, u32[]{:S(2)}) %collective-permute-start.25) | collective-permute-done | bytes 294944 | tf_op jit(solution)/shard_map/cond/branch_6_fun/ppermute | solution.py:170
  47.0 25.1 %collective-permute-done.26.back_ref = bf16[384,384]{1,0:T(8,128)(2,1)S(1)} collective-permute-done((bf16[384,384]{1,0:T(8,128)(2,1)}, bf16[384,384]{1,0:T(8,128)(2,1)S(1)}, u32[]{:S(2)}, u32[]{:S(2)}) %collective-permute-start.26) | collective-permute-done | bytes 294944 | tf_op jit(solution)/shard_map/cond/branch_6_fun/ppermute | solution.py:171
  72.1 0.0 all-to-all-done.6
  72.1 1.9 %collective-permute-start.27 = (bf16[3072,384]{1,0:T(8,128)(2,1)S(1)}, bf16[3072,384]{1,0:T(8,128)(2,1)S(1)}, u32[]{:S(2)}, u32[]{:S(2)}) collective-permute-start(bf16[3072,384]{1,0:T(8,128)(2,1)S(1)} %bitcast.74), channel_id=1, source_target_pairs={{0,32},{32,0},{1,33},{33,1},{2,34},{34,2},{3,35},{35,3},{4,36},{36... | collective-permute-start | bytes 7077896 | tf_op jit(solution)/shard_map/cond/branch_6_fun/ppermute | solution.py:174
  74.0 5.3 %branch_6_fun.2 = (bf16[16,192,384]{2,1,0:T(8,128)(2,1)S(1)}, bf16[16,192,384]{2,1,0:T(8,128)(2,1)S(1)}) custom-call(bf16[3072,384]{1,0:T(8,128)(2,1)S(1)} %bitcast.75, bf16[384,384]{1,0:T(8,128)(2,1)S(1)} %collective-permute-done.25.fwd_ref), custom_call_target="tpu_custom_call" | custom-call | flops 2000000000 | bytes 7000000 | tf_op jit(solution)/shard_map/cond/branch_6_fun/pallas_call | solution.py:103
  79.4 0.0 collective-permute-done.27.other_ref
  79.4 13.3 %branch_6_fun.3 = f32[16,16]{1,0:T(8,128)S(1)} custom-call(s32[1]{0:T(128)} %bitcast.30.core_ref, bf16[16,192,384]{2,1,0:T(8,128)(2,1)S(1)} %get-tuple-element.147.coef_mine_ref, bf16[16,192,384]{2,1,0:T(8,128)(2,1)S(1)} %get-tuple-element.148.left_mine_ref, bf16[3072,384]{1,0:T(8,128)(2,1)S(1)} %collective-permute-done.27.other_ref, ...), custom_call_target="tpu_custom_call" | custom-call | flops 5000000000 | bytes 10000000 | tf_op jit(solution)/shard_map/cond/branch_6_fun/pallas_call | solution.py:117
  93.0 0.6 broadcast_in_dim.90
  93.6 15.0 %all-to-all-start.9 = ((f32[16,2,16]{2,1,0:T(2,128)}), f32[16,2,16]{2,1,0:T(2,128)S(1)}, u32[]{:S(2)}, u32[]{:S(2)}) async-start(f32[16,2,16]{2,1,0:T(2,128)} %bitcast.55), calls=%async_computation.9 | async-start | bytes 32768 | tf_op jit(solution)/shard_map/all_to_all | solution.py:186
  108.6 0.6 dynamic_slice.6
  110.5 0.1 copy.23
  110.6 0.1 copy.25
  111.3 0.0 copy-done
  111.3 0.2 dynamic-slice_reduce_fusion
  111.5 8.4 %all-to-all-done.9 = f32[16,2,16]{2,1,0:T(2,128)S(1)} async-done(((f32[16,2,16]{2,1,0:T(2,128)}), f32[16,2,16]{2,1,0:T(2,128)S(1)}, u32[]{:S(2)}, u32[]{:S(2)}) %all-to-all-start.9) | async-done | bytes 2080 | tf_op jit(solution)/shard_map/all_to_all | solution.py:186
  119.9 0.6 broadcast_in_dim.91
  120.5 8.8 %all-to-all-start.10 = ((f32[32,1,16]{2,1,0:T(1,128)}), f32[32,1,16]{2,1,0:T(1,128)S(1)}, u32[]{:S(2)}, u32[]{:S(2)}) async-start(f32[32,1,16]{2,1,0:T(1,128)} %bitcast.56), calls=%async_computation.10 | async-start | bytes 32768 | tf_op jit(solution)/shard_map/all_to_all | solution.py:190
  129.4 0.1 multiply_reduce_fusion
  129.5 6.6 %all-to-all-done.10 = f32[32,1,16]{2,1,0:T(1,128)S(1)} async-done(((f32[32,1,16]{2,1,0:T(1,128)}), f32[32,1,16]{2,1,0:T(1,128)S(1)}, u32[]{:S(2)}, u32[]{:S(2)}) %all-to-all-start.10) | async-done | bytes 2080 | tf_op jit(solution)/shard_map/all_to_all | solution.py:190
  136.1 0.1 copy.27
  136.1 0.7 multiply_reduce_fusion.1
  (6 shorter events, 0.0 us)
Async XLA Ops:
  0.0 111.3 %copy-start = (f32[2,128,32]{1,2,0:T(8,128)S(1)}, f32[2,128,32]{1,2,0:T(8,128)}, u32[]{:S(2)}) copy-start(f32[2,128,32]{1,2,0:T(8,128)} %param.20) | copy-start | bytes 98308
  0.7 107.9 %copy-start.11 = (s32[32]{0:T(128)S(1)}, s32[32]{0:T(128)}, u32[]{:S(2)}) copy-start(s32[32]{0:T(128)} %param.22) | copy-start | bytes 388
  0.7 109.8 %copy-start.1 = (f32[32,32]{1,0:T(8,128)S(1)}, f32[32,32]{1,0:T(8,128)}, u32[]{:S(2)}) copy-start(f32[32,32]{1,0:T(8,128)} %param.21) | copy-start | bytes 12292
  0.9 20.2 %collective-permute-start.24 = (bf16[192,384]{1,0:T(8,128)(2,1)}, bf16[192,384]{1,0:T(8,128)(2,1)S(1)}, u32[]{:S(2)}, u32[]{:S(2)}) collective-permute-start(bf16[192,384]{1,0:T(8,128)(2,1)} %bitcast.117), channel_id=1, source_target_pairs={{0,0},{4,32},{32,4},{36,36},{1,1},{5,33},{33,5},{37,37},{2,2},{6,3... | collective-permute-start | bytes 442376 | tf_op jit(solution)/shard_map/cond/branch_6_fun/ppermute | solution.py:169
  22.8 6.9 %copy-start.8 = (bf16[384,384]{1,0:T(8,128)(2,1)S(1)}, bf16[384,384]{1,0:T(8,128)(2,1)}, u32[]{:S(2)}) copy-start(bf16[384,384]{1,0:T(8,128)(2,1)} %get-tuple-element.143) | copy-start | bytes 884740 | tf_op jit(solution)/shard_map/cond
  22.8 49.4 %all-to-all-start.6 = ((bf16[16,192,384]{2,1,0:T(8,128)(2,1)}), bf16[16,192,384]{2,1,0:T(8,128)(2,1)S(1)}, u32[]{:S(2)}, u32[]{:S(2)}) async-start(bf16[16,192,384]{2,1,0:T(8,128)(2,1)} %broadcast_in_dim.70), calls=%async_computation.6 | async-start | bytes 4718592 | tf_op jit(solution)/shard_map/cond/branch_6_fun/all_to_all | solution.py:138
  29.7 17.4 %collective-permute-start.25 = (bf16[384,384]{1,0:T(8,128)(2,1)S(1)}, bf16[384,384]{1,0:T(8,128)(2,1)S(1)}, u32[]{:S(2)}, u32[]{:S(2)}) collective-permute-start(bf16[384,384]{1,0:T(8,128)(2,1)S(1)} %copy-done.8), channel_id=1, source_target_pairs={{0,0},{4,32},{32,4},{36,36},{1,1},{5,33},{33,5},{37,37},{2,2},{6,3... | collective-permute-start | bytes 884744 | tf_op jit(solution)/shard_map/cond/branch_6_fun/ppermute | solution.py:170
  42.3 29.8 %collective-permute-start.26 = (bf16[384,384]{1,0:T(8,128)(2,1)}, bf16[384,384]{1,0:T(8,128)(2,1)S(1)}, u32[]{:S(2)}, u32[]{:S(2)}) collective-permute-start(bf16[384,384]{1,0:T(8,128)(2,1)} %get-tuple-element.144), channel_id=1, source_target_pairs={{224,0},{228,32},{128,4},{132,36},{160,64},{164,96},{192,68},{196,... | collective-permute-start | bytes 884744 | tf_op jit(solution)/shard_map/cond/branch_6_fun/ppermute | solution.py:171
  72.1 7.3 %collective-permute-start.27 = (bf16[3072,384]{1,0:T(8,128)(2,1)S(1)}, bf16[3072,384]{1,0:T(8,128)(2,1)S(1)}, u32[]{:S(2)}, u32[]{:S(2)}) collective-permute-start(bf16[3072,384]{1,0:T(8,128)(2,1)S(1)} %bitcast.74), channel_id=1, source_target_pairs={{0,32},{32,0},{1,33},{33,1},{2,34},{34,2},{3,35},{35,3},{4,36},{36... | collective-permute-start | bytes 7077896 | tf_op jit(solution)/shard_map/cond/branch_6_fun/ppermute | solution.py:174
  93.6 26.3 %all-to-all-start.9 = ((f32[16,2,16]{2,1,0:T(2,128)}), f32[16,2,16]{2,1,0:T(2,128)S(1)}, u32[]{:S(2)}, u32[]{:S(2)}) async-start(f32[16,2,16]{2,1,0:T(2,128)} %bitcast.55), calls=%async_computation.9 | async-start | bytes 32768 | tf_op jit(solution)/shard_map/all_to_all | solution.py:186
  120.5 15.6 %all-to-all-start.10 = ((f32[32,1,16]{2,1,0:T(1,128)}), f32[32,1,16]{2,1,0:T(1,128)S(1)}, u32[]{:S(2)}, u32[]{:S(2)}) async-start(f32[32,1,16]{2,1,0:T(1,128)} %bitcast.56), calls=%async_computation.10 | async-start | bytes 32768 | tf_op jit(solution)/shard_map/all_to_all | solution.py:190

commit v3 on v2

v3 whole, which is shorter than its diff:
```python
import functools

import jax
import jax.numpy as jnp
from jax import lax
from jax.experimental import pallas as pl
from jax.experimental.pallas import tpu as pltpu
from jax.sharding import Mesh
from jax.sharding import PartitionSpec as P

SIDE = 4
TILE = 16
POINTS = 16
VMEM_LIMIT = 24 * 1024 * 1024
COST = pl.CostEstimate(flops=1000, bytes_accessed=1000, transcendentals=0)


def onehot(rows, columns):
    return (rows == columns).astype(jnp.float32).astype(jnp.bfloat16)


def swap_order(blocks):
    size = TILE * blocks
    at = lax.broadcasted_iota(jnp.int32, (size, size), 0)
    source = lax.broadcasted_iota(jnp.int32, (size, size), 1)
    return onehot(at % TILE * blocks + at // TILE, source)


def ordered(order, piece_ref, group, blocks):
    size = TILE * blocks
    piece = piece_ref[pl.ds(pl.multiple_of(group * size, size), size), :]
    return jnp.dot(order, piece, preferred_element_type=jnp.float32).astype(jnp.bfloat16)


def left_kernel(piece_ref, fwd_ref, coef_ref, left_ref):
    blocks = coef_ref.shape[0]
    width = fwd_ref.shape[-1]
    order = swap_order(blocks)
    step = 3

    @pl.loop(0, coef_ref.shape[1] // TILE // step)
    def _(turn):
        coefs = []
        for part in range(step):
            group = turn * step + part
            coef = ordered(order, piece_ref, group, blocks)
            spot = pl.ds(pl.multiple_of(group * TILE, TILE), TILE)
            coef_ref[:, spot, :] = coef.reshape(blocks, TILE, width)
            coefs.append(coef)
        left = jnp.dot(
            jnp.concatenate(coefs, axis=0), fwd_ref[...], preferred_element_type=jnp.float32
        )
        left = left.astype(jnp.bfloat16).reshape(step, blocks, TILE, width)
        for part in range(step):
            group = turn * step + part
            spot = pl.ds(pl.multiple_of(group * TILE, TILE), TILE)
            left_ref[:, spot, :] = left[part]


def product_kernel(
    core_ref, coef_mine_ref, coef_other_ref, left_mine_ref, left_other_ref, upper_ref, lower_ref, out_ref, back_t_ref, right_ref
):
    blocks, half, width = coef_mine_ref.shape
    core = core_ref[0]
    run = 3 * TILE

    def picked(side):
        starts = [pl.multiple_of(y * 2 * run + side * run, TILE) for y in range(SIDE // 2)]
        refs = (upper_ref, lower_ref)
        return jnp.concatenate([ref[pl.ds(at, run), :] for ref in refs for at in starts], axis=0)

    back_t_ref[...] = jnp.concatenate([picked(core), picked(1 - core)], axis=0).T

    @pl.loop(0, blocks // 2)
    def _(pair):
        coefs = []
        for p in (2 * pair, 2 * pair + 1):
            coefs.append(jnp.concatenate([coef_mine_ref[p], coef_other_ref[p]], axis=0))
        right = jnp.dot(
            back_t_ref[...], jnp.concatenate(coefs, axis=1), preferred_element_type=jnp.float32
        )
        right = right.astype(jnp.bfloat16)
        right_ref[2 * pair] = right[:, :width]
        right_ref[2 * pair + 1] = right[:, width:]

    size = TILE * blocks
    gram = jnp.zeros((size, size), jnp.float32)
    for side, lefts in ((core, left_mine_ref), (1 - core, left_other_ref)):
        for y in range(SIDE):
            left_parts, right_parts = [], []
            for part in range(run // TILE):
                at = y * run + part * TILE
                natural = pl.multiple_of(y * 2 * run + side * run + part * TILE, TILE)
                left_parts.append(lefts[:, at : at + TILE, :].reshape(size, width))
                right_parts.append(right_ref[:, pl.ds(natural, TILE), :].reshape(size, width))
            gram += lax.dot_general(
                jnp.concatenate(left_parts, axis=1),
                jnp.concatenate(right_parts, axis=1),
                (((1,), (1,)), ((), ())),
                preferred_element_type=jnp.float32,
            )
    row = lax.broadcasted_iota(jnp.int32, (size, size), 0) % TILE
    column = lax.broadcasted_iota(jnp.int32, (size, size), 1) % TILE
    gram = jnp.where(row == column, gram, 0.0)
    gram = jnp.sum(gram.reshape(blocks, TILE, size), axis=1)
    at = lax.broadcasted_iota(jnp.int32, (size, blocks), 0) // TILE
    which = lax.broadcasted_iota(jnp.int32, (size, blocks), 1)
    pick = (at == which).astype(jnp.float32)
    polar = jnp.dot(gram, pick, precision=lax.Precision.HIGHEST, preferred_element_type=jnp.float32)
    out_ref[...] = polar * (-1.0 / POINTS)


def left_half(piece, green_fwd, blocks):
    width = green_fwd.shape[-1]
    shape = jax.ShapeDtypeStruct((blocks, piece.shape[0] // blocks, width), jnp.bfloat16)
    return pl.pallas_call(
        left_kernel,
        out_shape=(shape, shape),
        in_specs=[pl.BlockSpec(memory_space=pltpu.VMEM)] * 2,
        out_specs=[pl.BlockSpec(memory_space=pltpu.VMEM)] * 2,
        compiler_params=pltpu.CompilerParams(vmem_limit_bytes=VMEM_LIMIT),
        cost_estimate=COST,
    )(piece, green_fwd)


def product(core, coef_mine, coef_other, left_mine, left_other, upper, lower):
    blocks, half, width = coef_mine.shape
    return pl.pallas_call(
        product_kernel,
        out_shape=jax.ShapeDtypeStruct((blocks, blocks), jnp.float32),
        in_specs=[pl.BlockSpec(memory_space=pltpu.SMEM)]
        + [pl.BlockSpec(memory_space=pltpu.VMEM)] * 6,
        out_specs=pl.BlockSpec(memory_space=pltpu.VMEM),
        scratch_shapes=[
            pltpu.VMEM((width, width), jnp.bfloat16),
            pltpu.VMEM((blocks, width, width), jnp.bfloat16),
        ],
        compiler_params=pltpu.CompilerParams(vmem_limit_bytes=VMEM_LIMIT),
        cost_estimate=COST,
    )(core, coef_mine, coef_other, left_mine, left_other, upper, lower)


def spread(block, axes, count):
    copies = jnp.broadcast_to(block[None], (count,) + block.shape)
    return lax.all_to_all(copies, axes, 0, 0, tiled=True)


def shards(sizes, bcoef, fwd_green, back_green, kmq, ir_table, ir_fit, freq_index):
    zl, cores, ys, zh, xs = (sizes[name] for name in ("zl", "c", "y", "zh", "x"))
    blocks, rows, orb = bcoef.shape[1:]
    points = zl * cores
    minor = points // SIDE
    core = lax.axis_index("c")
    high = lax.axis_index("zh")
    low = lax.axis_index("zl")
    here_y, here_x = lax.axis_index("y"), lax.axis_index("x")

    own_k = low * cores + core
    target = kmq[0]
    major_shift = ((own_k >> 2) - (target >> 2)) & 3
    minor_shift = ((own_k & 3) - (target & 3)) & 3
    branch = (major_shift - 1) * (minor - 1) + minor_shift - 1

    transposed = [(c * zh + h, h * zh + c) for c in range(cores) for h in range(zh)]

    def partner(major, minor_by):
        route = []
        for k in range(points):
            a, b = divmod(k, minor)
            source = (a - major) % SIDE * minor + (b - minor_by) % minor
            for h in range(zh):
                route.append((source * zh + h, (k // cores * cores + h) * zh + k % cores))

        def work(shard, green_fwd, green_back):
            shard = shard.transpose(1, 0, 2).reshape(rows * blocks, orb)
            shard = lax.ppermute(shard, ("c", "zh"), transposed)
            green_fwd = lax.ppermute(green_fwd, ("c", "zh"), transposed)
            upper, lower = green_back[: orb // 2], green_back[orb // 2 :]
            upper = lax.ppermute(upper, ("zl", "c", "zh"), route)
            lower = lax.ppermute(lower, ("zl", "c", "zh"), route)
            mine = lax.cond(
                target >= 0,
                lambda block: spread(block, ("y", "x"), ys * xs),
                lambda block: jnp.zeros((ys * xs,) + block.shape, block.dtype),
                shard,
            )
            mine = mine.reshape(ys * xs * rows * blocks, orb)
            mine, green_fwd, upper = lax.optimization_barrier((mine, green_fwd, upper))
            other = lax.ppermute(mine, "c", [(0, 1), (1, 0)])
            coef_mine, left_mine = left_half(mine, green_fwd, blocks)
            coef_other, left_other = left_half(other, green_fwd, blocks)
            return product(core[None], coef_mine, coef_other, left_mine, left_other, upper, lower)

        return work

    works = [partner(a, b) for a in range(1, SIDE) for b in range(1, minor)]
    polar = lax.switch(branch, works, bcoef[0], fwd_green[0, 0], back_green[0, 0])

    pairs = polar.reshape(zl, 1, cores, blocks)
    pairs = jnp.broadcast_to(pairs, (zl, zh, cores, blocks)).reshape(zl * zh, cores, blocks)
    parts = lax.all_to_all(pairs, ("zl", "zh"), 0, 0, tiled=True)
    summed = jnp.sum(parts, axis=0)
    entries = jnp.broadcast_to(summed[:, None, :], (cores, ys * xs, blocks))
    entries = entries.reshape(cores * ys * xs, blocks)
    times = lax.all_to_all(entries, ("c", "y", "x"), 0, 0, tiled=True)

    own_w = (here_y * zh + high) * xs + here_x
    chosen = lax.dynamic_slice_in_dim(ir_table, freq_index[own_w], 1, axis=1)
    fit = ir_fit.reshape(-1, ys, cores, xs).transpose(0, 2, 1, 3).reshape(ir_fit.shape)
    transform = jnp.sum(chosen.transpose(0, 2, 1) * fit[None], axis=1)
    result = jnp.sum(transform[:, :, None] * times[None], axis=1)
    return result[:, None, None, :]


def solution(mesh):
    sizes = {"zl": 8, "c": 2, "y": 4, "zh": 2, "x": 4}
    fine = Mesh(mesh.devices.reshape(tuple(sizes.values())), tuple(sizes))
    ka, tau = ("zl", "c"), ("y", "zh", "x")
    return jax.shard_map(
        functools.partial(shards, sizes),
        mesh=fine,
        in_specs=(
            P(ka, None, tau, None),
            P(ka, tau, None, None),
            P(ka, tau, None, None),
            P(ka),
            P(),
            P(),
            P(),
        ),
        out_specs=P(None, tau, ka, None),
        check_vma=False,
    )
```

time: 137 us -> 126 us (0.920)
  waiting for transfers between devices: 46.2 us -> 15.2 us
  blocking collectives: 0 us -> 30 us
  starting transfers between devices: 64.1 us -> 56.6 us
  Pallas kernels: 18.6 us -> 11.6 us
  loops' own time: 0.54 us -> 5.25 us
    all_to_all x0 -> x1, blocking collectives: none -> 30 us  [spread(): return lax.all_to_all(copies, axes, 0, 0, tiled=True)]
    ppermute x1 -> x2, waiting for transfers between devices: 25.1 us -> 0.01 us  [the longest x1 0.01 us: work(): upper = lax.ppermute(upper, ('zl', 'c', 'zh'), route)]
    ppermute x1, starting transfers between devices: 12.7 us -> 1.92 us  [work(): green_fwd = lax.ppermute(green_fwd, ('c', 'zh'), transposed)]
    ppermute x1, starting transfers between devices: 1.91 us -> 11 us  [work(): other = lax.ppermute(mine, 'c', [(0, 1), (1, 0)])]
    pallas_call x1, Pallas kernels: 13.3 us -> 5.7 us  [product(): pl.pallas_call(product_kernel, out_shape=jax.ShapeDtypeStruct((blocks, bl...]
    all_to_all x1 -> x0, starting transfers between devices: 6.89 us -> none  [spread(): return lax.all_to_all(copies, axes, 0, 0, tiled=True)]
    ppermute x1 -> x2, starting transfers between devices: 1.92 us -> 8.08 us  [the longest x1 6.16 us: work(): lower = lax.ppermute(lower, ('zl', 'c', 'zh'), route)]
    another operation x1, loops' own time: 0.54 us -> 5.22 us  [shards(): lax.switch(branch, works, bcoef[0], fwd_green[0, 0], back_green[0, 0])]
  transfers between devices with their start and end apart: 7 -> 7, of which waited for: 5 -> 2; matrix products, arithmetic and copies ran while one was open for 1% -> 2% of each run, Pallas kernels for 4% -> 5%
where the time goes in v3:
time: 126 us
  starting transfers between devices  56.6 us (45%)
  blocking collectives  30 us (24%)
  waiting for transfers between devices  15.2 us (12%)
  Pallas kernels  11.6 us (9%)
  loops' own time  5.25 us (4%)
  local copies, waits for them, and re-layouts  3.5 us (3%)
  between operations  2.67 us (2%)
    all_to_all x1, blocking collectives, spread(): return lax.all_to_all(copies, axes, 0, 0, tiled=True)  30 us
    ppermute x1, starting transfers between devices, work(): shard = lax.ppermute(shard, ('c', 'zh'), transposed)  16.8 us
    all_to_all x1, starting transfers between devices, shards(): parts = lax.all_to_all(pairs, ('zl', 'zh'), 0, 0, tiled=True)  12.6 us
    ppermute x1, starting transfers between devices, work(): other = lax.ppermute(mine, 'c', [(0, 1), (1, 0)])  11 us
    all_to_all x1, waiting for transfers between devices, shards(): parts = lax.all_to_all(pairs, ('zl', 'zh'), 0, 0, tiled=True)  8.44 us
    all_to_all x1, waiting for transfers between devices, shards(): times = lax.all_to_all(entries, ('c', 'y', 'x'), 0, 0, tiled=True)  6.73 us
    all_to_all x1, starting transfers between devices, shards(): times = lax.all_to_all(entries, ('c', 'y', 'x'), 0, 0, tiled=True)  6.17 us
    ppermute x1, starting transfers between devices, work(): lower = lax.ppermute(lower, ('zl', 'c', 'zh'), route)  6.16 us
  transfers between devices with their start and end apart: 7, of which 2 were waited for; matrix products, arithmetic and copies ran while one was open for 2% of the time, Pallas kernels for 5%

profile of v3, /device:TPU:1, one launch (start us, length us, event | category | flops | bytes accessed | tf_op | source)
XLA Modules:
  0.0 125.6 jit_solution(9564833907301725364)
XLA Ops:
  0.0 0.0 copy-start
  0.7 86.0 %conditional.10 = (f32[16,16]{1,0:T(8,128)S(1)}) conditional(s32[]{:T(128)} %clamp.3, (s32[]{:T(128)}, s32[]{:T(128)}, bf16[16,12,384]{2,0,1:T(8,128)(2,1)}, bf16[384,384]{1,0:T(8,128)(2,1)}, bf16[384,384]{1,0:T(8,128)(2,1)}) %tuple.168, (s32[]{:T(128)}, s32[]{:T(128)}, bf16[16,12,384]{2,0,1:T(8,128)(2,1)}, ...), branch_computations={%region_1.4_spmd, %region_4.7_spmd, %region_7.10_spmd, %region_10.... | conditional | flops 3002 | bytes 20204702 | solution.py:197
  4.7 16.8 %collective-permute-start.15 = (bf16[192,384]{1,0:T(8,128)(2,1)}, bf16[192,384]{1,0:T(8,128)(2,1)S(1)}, u32[]{:S(2)}, u32[]{:S(2)}) collective-permute-start(bf16[192,384]{1,0:T(8,128)(2,1)} %bitcast.106), channel_id=1, source_target_pairs={{0,0},{4,32},{32,4},{36,36},{1,1},{5,33},{33,5},{37,37},{2,2},{6,3... | collective-permute-start | bytes 442376 | tf_op jit(solution)/shard_map/cond/branch_3_fun/ppermute | solution.py:176
  21.5 1.9 %collective-permute-start.16 = (bf16[384,384]{1,0:T(8,128)(2,1)}, bf16[384,384]{1,0:T(8,128)(2,1)S(1)}, u32[]{:S(2)}, u32[]{:S(2)}) collective-permute-start(bf16[384,384]{1,0:T(8,128)(2,1)} %get-tuple-element.189), channel_id=1, source_target_pairs={{0,0},{4,32},{32,4},{36,36},{1,1},{5,33},{33,5},{37,37},{2,2},{6,3... | collective-permute-start | bytes 884744 | tf_op jit(solution)/shard_map/cond/branch_3_fun/ppermute | solution.py:177
  23.4 1.0 fusion.3
  24.5 1.9 %collective-permute-start.17 = (bf16[192,384]{1,0:T(8,128)(2,1)S(1)}, bf16[192,384]{1,0:T(8,128)(2,1)S(1)}, u32[]{:S(2)}, u32[]{:S(2)}) collective-permute-start(bf16[192,384]{1,0:T(8,128)(2,1)S(1)} %get-tuple-element.265), channel_id=1, source_target_pairs={{352,0},{356,32},{256,4},{260,36},{288,64},{292,96},{320,68},{324,... | collective-permute-start | bytes 442376 | tf_op jit(solution)/shard_map/cond/branch_3_fun/ppermute | solution.py:179
  27.0 0.0 collective-permute-done.15
  27.0 30.4 %conditional.3 = (bf16[3072,384]{1,0:T(8,128)(2,1)S(1)}) conditional(s32[]{:T(128)} %convert_element_type.21, () %tuple.92, bf16[192,384]{1,0:T(8,128)(2,1)S(1)} %collective-permute-done.15), branch_computations={%region_11.0_spmd, %region_12.12_spmd} | conditional | bytes 7225352 | solution.py:181
  27.1 0.3 broadcast_in_dim.53
  27.4 30.0 %all_to_all.53 = bf16[16,192,384]{2,1,0:T(8,128)(2,1)S(1)} all-to-all(bf16[16,192,384]{2,1,0:T(8,128)(2,1)S(1)} %broadcast_in_dim.53), channel_id=1, replica_groups=mesh['zl'=8,'c'=2,'y'=4,'zh'=2,'x'=4] {'y','x'}, dimensions={0} | all-to-all | bytes 4718592 | tf_op jit(solution)/shard_map/cond/branch_3_fun/cond/branch_1_fun/all_to_all | solution.py:145
  57.4 0.0 collective-permute-done.17.upper_ref
  57.4 0.0 collective-permute-done.16.fwd_ref
  57.4 11.0 %collective-permute-start.18 = (bf16[3072,384]{1,0:T(8,128)(2,1)S(1)}, bf16[3072,384]{1,0:T(8,128)(2,1)S(1)}, u32[]{:S(2)}, u32[]{:S(2)}) collective-permute-start(bf16[3072,384]{1,0:T(8,128)(2,1)S(1)} %get-tuple-element.279.piece_ref), channel_id=1, source_target_pairs={{0,32},{32,0},{1,33},{33,1},{2,34},{34,2},{3,35},{35,3},{4,36},{36... | collective-permute-start | bytes 7077896 | tf_op jit(solution)/shard_map/cond/branch_3_fun/ppermute | solution.py:189
  68.5 6.2 %collective-permute-start.19 = (bf16[192,384]{1,0:T(8,128)(2,1)S(1)}, bf16[192,384]{1,0:T(8,128)(2,1)S(1)}, u32[]{:S(2)}, u32[]{:S(2)}) collective-permute-start(bf16[192,384]{1,0:T(8,128)(2,1)S(1)} %get-tuple-element.264), channel_id=1, source_target_pairs={{352,0},{356,32},{256,4},{260,36},{288,64},{292,96},{320,68},{324,... | collective-permute-start | bytes 442376 | tf_op jit(solution)/shard_map/cond/branch_3_fun/ppermute | solution.py:180
  74.6 2.9 %branch_3_fun.3 = (bf16[16,192,384]{2,1,0:T(8,128)(2,1)S(1)}, bf16[16,192,384]{2,1,0:T(8,128)(2,1)S(1)}) custom-call(bf16[3072,384]{1,0:T(8,128)(2,1)S(1)} %get-tuple-element.279.piece_ref, bf16[384,384]{1,0:T(8,128)(2,1)S(1)} %collective-permute-done.16.fwd_ref), custom_call_target="tpu_custom_call" | custom-call | flops 1000 | bytes 1000 | tf_op jit(solution)/shard_map/cond/branch_3_fun/pallas_call | solution.py:116
  77.6 0.0 collective-permute-done.18.piece_ref
  77.6 2.9 %branch_3_fun.4 = (bf16[16,192,384]{2,1,0:T(8,128)(2,1)S(1)}, bf16[16,192,384]{2,1,0:T(8,128)(2,1)S(1)}) custom-call(bf16[3072,384]{1,0:T(8,128)(2,1)S(1)} %collective-permute-done.18.piece_ref, bf16[384,384]{1,0:T(8,128)(2,1)S(1)} %collective-permute-done.16.fwd_ref), custom_call_target="tpu_custom_call" | custom-call | flops 1000 | bytes 1000 | tf_op jit(solution)/shard_map/cond/branch_3_fun/pallas_call | solution.py:116
  80.5 0.0 collective-permute-done.19.lower_ref
  80.5 5.7 %branch_3_fun.5 = f32[16,16]{1,0:T(8,128)S(1)} custom-call(s32[1]{0:T(128)} %bitcast.16.core_ref, bf16[16,192,384]{2,1,0:T(8,128)(2,1)S(1)} %get-tuple-element.193.coef_mine_ref, bf16[16,192,384]{2,1,0:T(8,128)(2,1)S(1)} %get-tuple-element.194.coef_other_ref, bf16[16,192,384]{2,1,0:T(8,128)(2,1)S(1)} %get-tuple-element.195.left_mine_ref, ...), custom_call_target="tpu_custom_call" | custom-call | flops 1000 | bytes 1000 | tf_op jit(solution)/shard_map/cond/branch_3_fun/pallas_call | solution.py:128
  86.7 0.6 broadcast_in_dim.90
  87.4 12.6 %all-to-all-start.9 = ((f32[16,2,16]{2,1,0:T(2,128)}), f32[16,2,16]{2,1,0:T(2,128)S(1)}, u32[]{:S(2)}, u32[]{:S(2)}) async-start(f32[16,2,16]{2,1,0:T(2,128)} %bitcast.54), calls=%async_computation.9 | async-start | bytes 32768 | tf_op jit(solution)/shard_map/all_to_all | solution.py:201
  99.9 0.1 copy.23
  100.0 0.1 copy.25
  100.1 0.6 dynamic_slice.6
  102.7 0.2 dynamic-slice_reduce_fusion
  102.8 8.4 %all-to-all-done.9 = f32[16,2,16]{2,1,0:T(2,128)S(1)} async-done(((f32[16,2,16]{2,1,0:T(2,128)}), f32[16,2,16]{2,1,0:T(2,128)S(1)}, u32[]{:S(2)}, u32[]{:S(2)}) %all-to-all-start.9) | async-done | bytes 2080 | tf_op jit(solution)/shard_map/all_to_all | solution.py:201
  111.3 0.6 broadcast_in_dim.91
  111.9 6.2 %all-to-all-start.10 = ((f32[32,1,16]{2,1,0:T(1,128)}), f32[32,1,16]{2,1,0:T(1,128)S(1)}, u32[]{:S(2)}, u32[]{:S(2)}) async-start(f32[32,1,16]{2,1,0:T(1,128)} %bitcast.55), calls=%async_computation.10 | async-start | bytes 32768 | tf_op jit(solution)/shard_map/all_to_all | solution.py:205
  118.1 0.1 multiply_reduce_fusion
  118.2 6.7 %all-to-all-done.10 = f32[32,1,16]{2,1,0:T(1,128)S(1)} async-done(((f32[32,1,16]{2,1,0:T(1,128)}), f32[32,1,16]{2,1,0:T(1,128)S(1)}, u32[]{:S(2)}, u32[]{:S(2)}) %all-to-all-start.10) | async-done | bytes 2080 | tf_op jit(solution)/shard_map/all_to_all | solution.py:205
  124.9 0.1 copy.27
  125.0 0.7 multiply_reduce_fusion.1
  (7 shorter events, 0.0 us)
Async XLA Ops:
  0.0 102.6 %copy-start = (f32[2,128,32]{1,2,0:T(8,128)S(1)}, f32[2,128,32]{1,2,0:T(8,128)}, u32[]{:S(2)}) copy-start(f32[2,128,32]{1,2,0:T(8,128)} %param.38) | copy-start | bytes 98308
  0.7 99.3 %copy-start.1 = (f32[32,32]{1,0:T(8,128)S(1)}, f32[32,32]{1,0:T(8,128)}, u32[]{:S(2)}) copy-start(f32[32,32]{1,0:T(8,128)} %param.39) | copy-start | bytes 12292
  0.7 99.4 %copy-start.2 = (s32[32]{0:T(128)S(1)}, s32[32]{0:T(128)}, u32[]{:S(2)}) copy-start(s32[32]{0:T(128)} %param.40) | copy-start | bytes 388
  4.7 22.4 %collective-permute-start.15 = (bf16[192,384]{1,0:T(8,128)(2,1)}, bf16[192,384]{1,0:T(8,128)(2,1)S(1)}, u32[]{:S(2)}, u32[]{:S(2)}) collective-permute-start(bf16[192,384]{1,0:T(8,128)(2,1)} %bitcast.106), channel_id=1, source_target_pairs={{0,0},{4,32},{32,4},{36,36},{1,1},{5,33},{33,5},{37,37},{2,2},{6,3... | collective-permute-start | bytes 442376 | tf_op jit(solution)/shard_map/cond/branch_3_fun/ppermute | solution.py:176
  21.5 35.9 %collective-permute-start.16 = (bf16[384,384]{1,0:T(8,128)(2,1)}, bf16[384,384]{1,0:T(8,128)(2,1)S(1)}, u32[]{:S(2)}, u32[]{:S(2)}) collective-permute-start(bf16[384,384]{1,0:T(8,128)(2,1)} %get-tuple-element.189), channel_id=1, source_target_pairs={{0,0},{4,32},{32,4},{36,36},{1,1},{5,33},{33,5},{37,37},{2,2},{6,3... | collective-permute-start | bytes 884744 | tf_op jit(solution)/shard_map/cond/branch_3_fun/ppermute | solution.py:177
  24.5 33.0 %collective-permute-start.17 = (bf16[192,384]{1,0:T(8,128)(2,1)S(1)}, bf16[192,384]{1,0:T(8,128)(2,1)S(1)}, u32[]{:S(2)}, u32[]{:S(2)}) collective-permute-start(bf16[192,384]{1,0:T(8,128)(2,1)S(1)} %get-tuple-element.265), channel_id=1, source_target_pairs={{352,0},{356,32},{256,4},{260,36},{288,64},{292,96},{320,68},{324,... | collective-permute-start | bytes 442376 | tf_op jit(solution)/shard_map/cond/branch_3_fun/ppermute | solution.py:179
  57.4 20.2 %collective-permute-start.18 = (bf16[3072,384]{1,0:T(8,128)(2,1)S(1)}, bf16[3072,384]{1,0:T(8,128)(2,1)S(1)}, u32[]{:S(2)}, u32[]{:S(2)}) collective-permute-start(bf16[3072,384]{1,0:T(8,128)(2,1)S(1)} %get-tuple-element.279.piece_ref), channel_id=1, source_target_pairs={{0,32},{32,0},{1,33},{33,1},{2,34},{34,2},{3,35},{35,3},{4,36},{36... | collective-permute-start | bytes 7077896 | tf_op jit(solution)/shard_map/cond/branch_3_fun/ppermute | solution.py:189
  68.5 12.0 %collective-permute-start.19 = (bf16[192,384]{1,0:T(8,128)(2,1)S(1)}, bf16[192,384]{1,0:T(8,128)(2,1)S(1)}, u32[]{:S(2)}, u32[]{:S(2)}) collective-permute-start(bf16[192,384]{1,0:T(8,128)(2,1)S(1)} %get-tuple-element.264), channel_id=1, source_target_pairs={{352,0},{356,32},{256,4},{260,36},{288,64},{292,96},{320,68},{324,... | collective-permute-start | bytes 442376 | tf_op jit(solution)/shard_map/cond/branch_3_fun/ppermute | solution.py:180
  87.4 23.9 %all-to-all-start.9 = ((f32[16,2,16]{2,1,0:T(2,128)}), f32[16,2,16]{2,1,0:T(2,128)S(1)}, u32[]{:S(2)}, u32[]{:S(2)}) async-start(f32[16,2,16]{2,1,0:T(2,128)} %bitcast.54), calls=%async_computation.9 | async-start | bytes 32768 | tf_op jit(solution)/shard_map/all_to_all | solution.py:201
  111.9 13.0 %all-to-all-start.10 = ((f32[32,1,16]{2,1,0:T(1,128)}), f32[32,1,16]{2,1,0:T(1,128)S(1)}, u32[]{:S(2)}, u32[]{:S(2)}) async-start(f32[32,1,16]{2,1,0:T(1,128)} %bitcast.55), calls=%async_computation.10 | async-start | bytes 32768 | tf_op jit(solution)/shard_map/all_to_all | solution.py:205
